TPU v7x, 128 devices: a whole 4x4x4 slice. The times are simulated.
128 devices in a mesh: blk: 8 (over y_lo, x), vslab: 16 (over z, y_hi, core).
Axes of the slice: x: 4, y: 4 (y_hi: 2, y_lo: 2; y = y_hi * 2 + y_lo), z: 4, core: 2. Of those that a mesh axis runs over, the one named last changes fastest.
Arguments:
- amplitudes: float32 [1024, 128, 800], P('blk', 'vslab'), may hold values from -6 to 6
- integrals: float32 [128, 800, 4096], P('vslab', None, 'blk'), may hold values from -0.01953125 to 0.01953125
- ab_energy: float32 [4096], P('blk'), may hold values from 1 to 4
- ij_energy: float32 [1024], replicated, may hold values from -4 to -1
- block_size: int32 [32], replicated, may hold values from 1 to 95, as said below
- block_owner: int32 [32], replicated, may hold values from 0 to 15, as said below
Outputs:
- amplitude_new: float32 [1024, 12288], P(None, ('blk', 'vslab'))
Inputs may be any that keep to these rules, and one draw needn't show every extreme that they name: `block_size`: the blocks of one group fill its 512 pairs exactly; every owner holds at most 96 pairs, and one owner exactly 96. `block_owner`: every owner has two blocks.
All inputs are finite; a program needn't handle non-finite values.
Results may differ from a plain program's by a relative error of at most 0.00007.
Values sent between devices are 32-bit elements; how exact they have to be, the bound alone decides.
No kernel may reach another device: no remote copies, remote signals or barrier semaphores. Data moves between devices by JAX's collectives and lax.ppermute only.
A program may use at most 128 MiB of HBM per device.

v0:
```python
import jax
import jax.numpy as jnp
from jax import lax
from jax.experimental import pallas as pl
from jax.experimental.pallas import tpu as pltpu
from jax.sharding import PartitionSpec as P

NX, NY = 4, 2
STEPS = ((1, 0), (3, 0), (0, 1))
ROUNDS = (
    ((0, 1, (0, 0)), (1, 0, (0, 0)), (2, 0, (0, 0))),
    ((0, 0, (0, 0)), (1, 2, (0, 0)), (2, 1, (1, 0))),
    ((0, 2, (0, 0)), (1, 1, (1, 1)), (2, 2, (0, 0))),
    ((0, 2, (0, 1)), (1, 1, (0, 0)), (2, 0, (1, 0))),
    ((0, 1, (1, 0)), (1, 0, (3, 0)), (2, 1, (3, 0))),
    ((0, 2, (1, 0)), (1, 0, (0, 1)), (2, 2, (3, 0))),
    ((0, 0, (1, 1)), (1, 2, (3, 1)), (2, 1, (2, 0))),
)
BATCHES = (
    {"blocks": 1, "pack": 0, "core": 1, "near": 2, "far": 3},
    {"blocks": 2, "pack": 3, "core": 4, "near": 5, "far": 6},
    {"blocks": 2, "pack": 4, "core": 5, "near": 6},
    {"blocks": 2, "pack": 6},
    {"blocks": 1},
)
NEXT = ("pack", "core", "near", "far", "y")


def moved(offset, step):
    return ((offset[0] + step[0]) % NX, (offset[1] + step[1]) % NY)


def link_pairs(step):
    pairs = []
    for y in range(NY):
        for x in range(NX):
            to_x, to_y = moved((x, y), step)
            pairs.append((y * NX + x, to_y * NX + to_x))
    return pairs


def slot_of_pairs(block_size, block_owner, rows, cap):
    count = block_size.shape[0]
    order = jnp.arange(count, dtype=jnp.int32)
    earlier = order[None, :] < order[:, None]
    starts = jnp.sum(jnp.where(earlier, block_size[None, :], 0), axis=1)
    same = block_owner[:, None] == block_owner[None, :]
    before = jnp.sum(jnp.where(same & earlier, block_size[None, :], 0), axis=1)
    row_ids = jnp.arange(rows, dtype=jnp.int32)
    inside = (row_ids[:, None] >= starts[None, :]) & (
        row_ids[:, None] < (starts + block_size)[None, :]
    )
    base = block_owner * cap + before - starts
    return jnp.sum(jnp.where(inside, base[None, :], 0), axis=1) + row_ids


CHEAP = pl.CostEstimate(flops=1, bytes_accessed=1, transcendentals=0)
PARAMS = pltpu.CompilerParams(vmem_limit_bytes=14 * 2**20)
F32 = jnp.float32


def halves(x):
    high = x.astype(jnp.bfloat16)
    return high, (x - high.astype(F32)).astype(jnp.bfloat16)


def product_kernel(t_ref, v_ref, out_ref):
    t_high, t_low = halves(t_ref[...])
    v_high, v_low = halves(v_ref[...])

    def dot(t, v):
        return lax.dot_general(t, v, (((0,), (0,)), ((), ())), preferred_element_type=F32)

    term = dot(t_high, v_high) + (dot(t_high, v_low) + dot(t_low, v_high))

    @pl.when(pl.program_id(0) == 0)
    def _():
        out_ref[...] = term

    @pl.when(pl.program_id(0) > 0)
    def _():
        out_ref[...] += term


def product(t, v, first):
    depth, rows = t.shape
    steps = 4 if depth % 64 == 0 else 2
    tile, width = depth // steps, v.shape[1]
    return pl.pallas_call(
        product_kernel,
        grid=(steps,),
        in_specs=[
            pl.BlockSpec((tile, rows), lambda k: (k, 0)),
            pl.BlockSpec((pl.Element(tile), pl.Element(width)), lambda k: (pl.multiple_of(first + k * tile, 16), 0)),
        ],
        out_specs=pl.BlockSpec((rows, width), lambda k: (0, 0)),
        out_shape=jax.ShapeDtypeStruct((rows, width), F32),
        cost_estimate=CHEAP,
        compiler_params=PARAMS,
        name="product",
    )(t, v)


def pack_kernel(hot_ref, p_ref, out_ref):
    rest, total = p_ref[...], None
    for _ in range(3):
        part = rest.astype(jnp.bfloat16)
        rest = rest - part.astype(F32)
        term = lax.dot_general(hot_ref[...], part, (((1,), (1,)), ((), ())), preferred_element_type=F32)
        total = term if total is None else total + term
    out_ref[...] = total


def pack(hot, ladder):
    tile = hot.shape[0] // 4
    return pl.pallas_call(
        pack_kernel,
        grid=(4,),
        in_specs=[
            pl.BlockSpec((tile, hot.shape[1]), lambda k: (k, 0)),
            pl.BlockSpec(ladder.shape, lambda k: (0, 0)),
        ],
        out_specs=pl.BlockSpec((tile, ladder.shape[0]), lambda k: (k, 0)),
        out_shape=jax.ShapeDtypeStruct((hot.shape[0], ladder.shape[0]), F32),
        cost_estimate=CHEAP,
        compiler_params=PARAMS,
        name="pack",
    )(hot, ladder)


def on_device(amplitudes, integrals, ab_energy, ij_energy, block_size, block_owner):
    owners = lax.axis_size("vslab")
    ij_b = amplitudes.shape[0]
    rows = integrals.shape[2]
    cap = 3 * rows // owners
    v_matrix = integrals.reshape(-1, rows)
    t_own = amplitudes.transpose(1, 2, 0).reshape(-1, ij_b)
    depth = t_own.shape[0]
    cuts = [0, depth // 96 // 2 * 64, depth - depth // 96 * 32 - 32, depth]

    held = {(p, (0, 0)): t_own[cuts[p] : cuts[p + 1]] for p in range(3)}
    terms = {}

    dest = slot_of_pairs(block_size, block_owner, rows, cap)
    mine = lax.axis_index("vslab")
    slots = jnp.arange(cap, dtype=jnp.int32)
    apart = jnp.array([c + 4 * z + 2 * y for c in (0, 1) for z in (0, 2, 1, 3) for y in (0, 1)], jnp.int32)
    near = mine ^ apart

    def one_hot(owner):
        at = (owner[:, None] * cap + slots[None, :]).reshape(-1)
        return (at[:, None] == dest[None, :]).astype(jnp.bfloat16)

    hot = one_hot(near)
    my_hot = hot[:cap] > 0.5
    my_energy = jnp.sum(jnp.where(my_hot, ab_energy[None, :], 0.0), axis=1)
    my_valid = jnp.any(my_hot, axis=1)

    def multiply(piece, offset):
        term = product(held[piece, offset], v_matrix, cuts[piece])
        terms[offset] = terms[offset] + term if offset in terms else term

    def swap(part, bits):
        return lax.ppermute(part, "vslab", [(i, i ^ bits) for i in range(owners)])

    def fold(part, bits):
        middle = part.shape[0] // 2
        return part[:middle] + swap(part[middle:], bits)

    def sum_z(part):
        width = 2 * cap
        total = part[:width]
        for k, bits in enumerate((8, 4, 12)):
            total = total + swap(part[(k + 1) * width : (k + 2) * width], bits)
        return total

    def step(name, part):
        if name == "pack":
            return pack(hot, part)
        return fold(part, {"core": 1, "near": 4, "far": 8, "y": 2}[name])

    fresh = [(p, (0, 0)) for p in range(3)]
    count = {}
    parts, order = [], []

    def start_batches():
        while len(parts) < len(BATCHES):
            batch = [o for o in terms if count[o] == 3][: BATCHES[len(parts)]["blocks"]]
            if len(batch) < BATCHES[len(parts)]["blocks"]:
                break
            parts.append(jnp.concatenate([terms.pop(o) for o in batch], axis=0))
            order.extend(batch)

    for number, sends in enumerate(ROUNDS):
        arrived = {}
        for link, p, offset in sends:
            to = moved(offset, STEPS[link])
            arrived[p, to] = lax.ppermute(held[p, offset], "blk", link_pairs(STEPS[link]))
        for p, offset in fresh:
            multiply(p, offset)
            count[offset] = count.get(offset, 0) + 1
        start_batches()
        for i, batch in enumerate(BATCHES[: len(parts)]):
            for name in NEXT:
                if batch.get(name) == number:
                    parts[i] = step(name, parts[i])
        fresh = list(arrived)
        held.update(arrived)
        h_keys, t_keys = list(held), list(terms)
        h, t, parts = lax.optimization_barrier(([held[k] for k in h_keys], [terms[k] for k in t_keys], parts))
        held, terms = dict(zip(h_keys, h)), dict(zip(t_keys, t))
    for p, offset in fresh:
        multiply(p, offset)
        count[offset] = count.get(offset, 0) + 1
    start_batches()
    own, first, second, third, last = parts
    last = jnp.concatenate([third, step("pack", last)], axis=1)
    last, second, own, first = lax.optimization_barrier((last, second, own, first))
    last = step("core", last)
    second = step("far", second)
    last, second, own, first = lax.optimization_barrier((last, second, own, first))
    last = sum_z(last)
    settled = step("y", jnp.concatenate([own, first], axis=1))
    last, second, settled = lax.optimization_barrier((last, second, settled))
    parts = [settled, step("y", jnp.concatenate([second, last], axis=1))]

    me = lax.axis_index("blk")
    my_x, my_y = me % NX, me // NX
    everything = jnp.concatenate(parts, axis=1)
    place = [NX * dy + dx for dx, dy in order]
    place_of = jnp.array([place.index(k) for k in range(NX * NY)], jnp.int32)
    columns = []
    for source in range(NX * NY):
        dx = (my_x + NX - source % NX) % NX
        dy = (my_y + NY - source // NX) % NY
        start = place_of[dy * NX + dx] * ij_b
        columns.append(lax.dynamic_slice_in_dim(everything, start, ij_b, axis=1))
    full = jnp.concatenate(columns, axis=1)
    denom = my_energy[:, None] - ij_energy[None, :]
    return jnp.where(my_valid[:, None], full / denom, 0.0).T


def solution(mesh):
    placed = (P("blk", "vslab", None), P("vslab", None, "blk"), P("blk"), P(), P(), P())
    return jax.shard_map(
        on_device, mesh=mesh, in_specs=placed, out_specs=P(None, ("blk", "vslab")), check_vma=False
    )
```

profile of v0, /device:TPU:1, one launch (start us, length us, event | category | flops | bytes accessed | tf_op | source)
XLA Modules:
  0.0 232.0 jit_solution(5019960595672328194)
XLA Ops:
  0.0 2.3 slice.129.t_ref
  2.3 3.3 %collective-permute-start.1 = (f32[2112,128]{1,0:T(8,128)}, f32[2112,128]{1,0:T(8,128)}, u32[]{:S(2)}, u32[]{:S(2)}) collective-permute-start(f32[2112,128]{1,0:T(8,128)} %slice.129.t_ref), channel_id=1, source_target_pairs={{0,48},{16,0},{32,16},{48,32},{64,112},{80,64},{96,80},{112,96},{1... | collective-permute-start | bytes 3244040 | tf_op jit(solution)/shard_map/ppermute | solution.py:198
  6.9 1.7 fusion.19
  9.0 4.7 %copy-done = f32[8,800,512]{2,1,0:T(8,128)S(1)} copy-done((f32[8,800,512]{2,1,0:T(8,128)S(1)}, f32[8,800,512]{2,1,0:T(8,128)}, u32[]{:S(2)}) %copy-start) | copy-done | bytes 13107224
  13.7 1.6 product.25
  15.3 3.6 %product.24 = f32[128,512]{1,0:T(8,128)S(1)} custom-call(f32[2112,128]{1,0:T(8,128)} %slice.129.t_ref, f32[6400,512]{1,0:T(8,128)S(1)} %bitcast.15), custom_call_target="tpu_custom_call" | custom-call | flops 1 | bytes 1 | tf_op jit(solution)/shard_map/product/pallas_call | solution.py:89
  18.9 1.6 product.26
  21.1 1.9 pack.5
  23.1 5.4 %collective-permute-done.1.t_ref = f32[2112,128]{1,0:T(8,128)} collective-permute-done((f32[2112,128]{1,0:T(8,128)}, f32[2112,128]{1,0:T(8,128)}, u32[]{:S(2)}, u32[]{:S(2)}) %collective-permute-start.1) | collective-permute-done | bytes 1081376 | tf_op jit(solution)/shard_map/ppermute | solution.py:198
  28.5 1.9 collective-permute-done.2.t_ref
  30.3 4.1 %collective-permute-done.t_ref = f32[2144,128]{1,0:T(8,128)} collective-permute-done((f32[2144,128]{1,0:T(8,128)S(1)}, f32[2144,128]{1,0:T(8,128)}, u32[]{:S(2)}, u32[]{:S(2)}) %collective-permute-start) | collective-permute-done | bytes 1097760 | tf_op jit(solution)/shard_map/ppermute | solution.py:198
  36.2 3.1 %collective-permute-start.6 = (f32[768,128]{1,0:T(8,128)S(1)}, f32[768,128]{1,0:T(8,128)S(1)}, u32[]{:S(2)}, u32[]{:S(2)}) collective-permute-start(f32[768,128]{1,0:T(8,128)S(1)} %slice.101), channel_id=1, source_target_pairs={{0,1},{1,0},{2,3},{3,2},{4,5},{5,4},{6,7},{7,6},{8,9},{9,8},{10,11... | collective-permute-start | bytes 1179656 | tf_op jit(solution)/shard_map/ppermute | solution.py:164
  39.2 4.7 %copy-done.1 = f32[8,800,512]{2,1,0:T(8,128)S(1)} copy-done((f32[8,800,512]{2,1,0:T(8,128)S(1)}, f32[8,800,512]{2,1,0:T(8,128)}, u32[]{:S(2)}) %copy-start.1) | copy-done | bytes 13107224
  44.0 2.6 %product.27 = f32[128,512]{1,0:T(8,128)S(1)} custom-call(f32[2144,128]{1,0:T(8,128)} %collective-permute-done.t_ref, f32[6400,512]{1,0:T(8,128)S(1)} %bitcast.17), custom_call_target="tpu_custom_call" | custom-call | flops 1 | bytes 1 | tf_op jit(solution)/shard_map/product/pallas_call | solution.py:89
  46.6 3.6 %product.28 = f32[128,512]{1,0:T(8,128)S(1)} custom-call(f32[2112,128]{1,0:T(8,128)} %collective-permute-done.1.t_ref, f32[6400,512]{1,0:T(8,128)S(1)} %bitcast.18), custom_call_target="tpu_custom_call" | custom-call | flops 1 | bytes 1 | tf_op jit(solution)/shard_map/product/pallas_call | solution.py:89
  50.2 3.6 %product.29 = f32[128,512]{1,0:T(8,128)S(1)} custom-call(f32[2112,128]{1,0:T(8,128)} %collective-permute-done.2.t_ref, f32[6400,512]{1,0:T(8,128)S(1)} %bitcast.19), custom_call_target="tpu_custom_call" | custom-call | flops 1 | bytes 1 | tf_op jit(solution)/shard_map/product/pallas_call | solution.py:89
  53.8 5.2 %collective-permute-done.3.t_ref = f32[2112,128]{1,0:T(8,128)S(1)} collective-permute-done((f32[2112,128]{1,0:T(8,128)}, f32[2112,128]{1,0:T(8,128)S(1)}, u32[]{:S(2)}, u32[]{:S(2)}) %collective-permute-start.3) | collective-permute-done | bytes 1081376 | tf_op jit(solution)/shard_map/ppermute | solution.py:198
  59.0 2.7 %collective-permute-start.8 = (f32[2144,128]{1,0:T(8,128)S(1)}, f32[2144,128]{1,0:T(8,128)S(1)}, u32[]{:S(2)}, u32[]{:S(2)}) collective-permute-start(f32[2144,128]{1,0:T(8,128)S(1)} %collective-permute-done.5.t_ref), channel_id=1, source_target_pairs={{0,48},{16,0},{32,16},{48,32},{64,112},{80,64},{96,80},{112,96},{1... | collective-permute-start | bytes 3293192 | tf_op jit(solution)/shard_map/ppermute | solution.py:198
  63.0 1.7 collective-permute-start.10
  64.7 1.6 product.32
  66.3 1.6 product.31
  67.9 2.2 product.30
  70.2 12.3 %collective-permute-done.7.t_ref = f32[2144,128]{1,0:T(8,128)S(1)} collective-permute-done((f32[2144,128]{1,0:T(8,128)S(1)}, f32[2144,128]{1,0:T(8,128)S(1)}, u32[]{:S(2)}, u32[]{:S(2)}) %collective-permute-start.7) | collective-permute-done | bytes 1097760 | tf_op jit(solution)/shard_map/ppermute | solution.py:198
  83.5 2.7 %collective-permute-start.12 = (f32[2144,128]{1,0:T(8,128)S(1)}, f32[2144,128]{1,0:T(8,128)S(1)}, u32[]{:S(2)}, u32[]{:S(2)}) collective-permute-start(f32[2144,128]{1,0:T(8,128)S(1)} %get-tuple-element.107.t_ref), channel_id=1, source_target_pairs={{0,48},{16,0},{32,16},{48,32},{64,112},{80,64},{96,80},{112,96},{1... | collective-permute-start | bytes 3293192 | tf_op jit(solution)/shard_map/ppermute | solution.py:198
  87.4 1.6 product.35
  89.1 1.6 product.33
  90.7 1.6 product.34
  92.3 3.7 %collective-permute-start.14 = (f32[192,128]{1,0:T(8,128)S(1)}, f32[192,128]{1,0:T(8,128)S(1)}, u32[]{:S(2)}, u32[]{:S(2)}) collective-permute-start(f32[192,128]{1,0:T(8,128)S(1)} %slice.105), channel_id=1, source_target_pairs={{0,8},{1,9},{2,10},{3,11},{4,12},{5,13},{6,14},{7,15},{8,0},{9,1},... | collective-permute-start | bytes 294920 | tf_op jit(solution)/shard_map/ppermute | solution.py:164
  96.1 2.1 pack.6
  98.3 7.8 %collective-permute-done.13.t_ref = f32[2112,128]{1,0:T(8,128)S(1)} collective-permute-done((f32[2112,128]{1,0:T(8,128)S(1)}, f32[2112,128]{1,0:T(8,128)S(1)}, u32[]{:S(2)}, u32[]{:S(2)}) %collective-permute-start.13) | collective-permute-done | bytes 1081376 | tf_op jit(solution)/shard_map/ppermute | solution.py:198
  107.5 2.6 %collective-permute-start.16 = (f32[2112,128]{1,0:T(8,128)}, f32[2112,128]{1,0:T(8,128)S(1)}, u32[]{:S(2)}, u32[]{:S(2)}) collective-permute-start(f32[2112,128]{1,0:T(8,128)} %collective-permute-done.1.t_ref), channel_id=1, source_target_pairs={{0,48},{16,0},{32,16},{48,32},{64,112},{80,64},{96,80},{112,96},{1... | collective-permute-start | bytes 3244040 | tf_op jit(solution)/shard_map/ppermute | solution.py:198
  110.1 10.3 %collective-permute-start.18 = (f32[768,256]{1,0:T(8,128)S(1)}, f32[768,256]{1,0:T(8,128)S(1)}, u32[]{:S(2)}, u32[]{:S(2)}) collective-permute-start(f32[768,256]{1,0:T(8,128)S(1)} %slice.107), channel_id=1, source_target_pairs={{0,1},{1,0},{2,3},{3,2},{4,5},{5,4},{6,7},{7,6},{8,9},{9,8},{10,11... | collective-permute-start | bytes 2359304 | tf_op jit(solution)/shard_map/ppermute | solution.py:164
  120.5 1.6 product.36
  122.1 1.6 product.37
  123.7 2.2 product.38
  126.0 2.1 pack.7
  130.4 2.4 %collective-permute-start.20 = (f32[2112,128]{1,0:T(8,128)}, f32[2112,128]{1,0:T(8,128)S(1)}, u32[]{:S(2)}, u32[]{:S(2)}) collective-permute-start(f32[2112,128]{1,0:T(8,128)} %collective-permute-done.2.t_ref), channel_id=1, source_target_pairs={{0,48},{16,0},{32,16},{48,32},{64,112},{80,64},{96,80},{112,96},{1... | collective-permute-start | bytes 3244040 | tf_op jit(solution)/shard_map/ppermute | solution.py:198
  132.8 11.8 %collective-permute-start.23 = (f32[768,256]{1,0:T(8,128)S(1)}, f32[768,256]{1,0:T(8,128)S(1)}, u32[]{:S(2)}, u32[]{:S(2)}) collective-permute-start(f32[768,256]{1,0:T(8,128)S(1)} %slice.111), channel_id=1, source_target_pairs={{0,1},{1,0},{2,3},{3,2},{4,5},{5,4},{6,7},{7,6},{8,9},{9,8},{10,11... | collective-permute-start | bytes 2359304 | tf_op jit(solution)/shard_map/ppermute | solution.py:164
  144.6 1.7 collective-permute-start.22
  146.3 1.6 product.39
  148.0 2.2 product.40
  150.2 1.6 product.41
  151.8 3.9 %collective-permute-done.22 = f32[384,256]{1,0:T(8,128)S(1)} collective-permute-done((f32[384,256]{1,0:T(8,128)S(1)}, f32[384,256]{1,0:T(8,128)S(1)}, u32[]{:S(2)}, u32[]{:S(2)}) %collective-permute-start.22) | collective-permute-done | bytes 393248 | tf_op jit(solution)/shard_map/ppermute | solution.py:164
  157.5 1.6 product.44
  159.1 2.2 product.43
  161.3 1.6 collective-permute-start.28
  163.0 3.4 %collective-permute-start.27 = (f32[192,256]{1,0:T(8,128)S(1)}, f32[192,256]{1,0:T(8,128)S(1)}, u32[]{:S(2)}, u32[]{:S(2)}) collective-permute-start(f32[192,256]{1,0:T(8,128)S(1)} %slice.113), channel_id=1, source_target_pairs={{0,8},{1,9},{2,10},{3,11},{4,12},{5,13},{6,14},{7,15},{8,0},{9,1},... | collective-permute-start | bytes 589832 | tf_op jit(solution)/shard_map/ppermute | solution.py:164
  166.5 1.6 product.42
  168.2 2.1 pack.8
  170.2 3.3 %collective-permute-done.27 = f32[192,256]{1,0:T(8,128)S(1)} collective-permute-done((f32[192,256]{1,0:T(8,128)S(1)}, f32[192,256]{1,0:T(8,128)S(1)}, u32[]{:S(2)}, u32[]{:S(2)}) %collective-permute-start.27) | collective-permute-done | bytes 196640 | tf_op jit(solution)/shard_map/ppermute | solution.py:164
  173.7 1.6 collective-permute-done.24.t_ref
  175.2 2.4 %collective-permute-done.25.t_ref = f32[2144,128]{1,0:T(8,128)S(1)} collective-permute-done((f32[2144,128]{1,0:T(8,128)S(1)}, f32[2144,128]{1,0:T(8,128)S(1)}, u32[]{:S(2)}, u32[]{:S(2)}) %collective-permute-start.25) | collective-permute-done | bytes 1097760 | tf_op jit(solution)/shard_map/ppermute | solution.py:198
  177.6 2.2 product.45
  179.8 1.6 product.46
  181.4 1.6 product.47
  183.1 1.9 pack.9
  185.3 6.1 %collective-permute-start.29 = (f32[768,384]{1,0:T(8,128)S(1)}, f32[768,384]{1,0:T(8,128)S(1)}, u32[]{:S(2)}, u32[]{:S(2)}) collective-permute-start(f32[768,384]{1,0:T(8,128)S(1)} %slice.117), channel_id=1, source_target_pairs={{0,1},{1,0},{2,3},{3,2},{4,5},{5,4},{6,7},{7,6},{8,9},{9,8},{10,11... | collective-permute-start | bytes 3538952 | tf_op jit(solution)/shard_map/ppermute | solution.py:164
  191.5 3.4 %collective-permute-start.30 = (f32[192,256]{1,0:T(8,128)S(1)}, f32[192,256]{1,0:T(8,128)S(1)}, u32[]{:S(2)}, u32[]{:S(2)}) collective-permute-start(f32[192,256]{1,0:T(8,128)S(1)} %slice.119), channel_id=1, source_target_pairs={{0,8},{1,9},{2,10},{3,11},{4,12},{5,13},{6,14},{7,15},{8,0},{9,1},... | collective-permute-start | bytes 589832 | tf_op jit(solution)/shard_map/ppermute | solution.py:164
  194.9 5.3 %collective-permute-done.30 = f32[192,256]{1,0:T(8,128)S(1)} collective-permute-done((f32[192,256]{1,0:T(8,128)S(1)}, f32[192,256]{1,0:T(8,128)S(1)}, u32[]{:S(2)}, u32[]{:S(2)}) %collective-permute-start.30) | collective-permute-done | bytes 196640 | tf_op jit(solution)/shard_map/ppermute | solution.py:164
  200.4 2.9 %collective-permute-start.34 = (f32[96,384]{1,0:T(8,128)S(1)}, f32[96,384]{1,0:T(8,128)S(1)}, u32[]{:S(2)}, u32[]{:S(2)}) collective-permute-start(f32[96,384]{1,0:T(8,128)S(1)} %slice.133), channel_id=1, source_target_pairs={{0,2},{1,3},{2,0},{3,1},{4,6},{5,7},{6,4},{7,5},{8,10},{9,11},{10,... | collective-permute-start | bytes 442376 | tf_op jit(solution)/shard_map/ppermute | solution.py:164
  204.2 2.8 %collective-permute-start.31 = (f32[192,384]{1,0:T(8,128)}, f32[192,384]{1,0:T(8,128)}, u32[]{:S(2)}, u32[]{:S(2)}) collective-permute-start(f32[192,384]{1,0:T(8,128)} %get-tuple-element.175), channel_id=1, source_target_pairs={{0,8},{1,9},{2,10},{3,11},{4,12},{5,13},{6,14},{7,15},{8,0},{9,1},... | collective-permute-start | bytes 884744 | tf_op jit(solution)/shard_map/ppermute | solution.py:164
  207.8 5.9 %collective-permute-done.31 = f32[192,384]{1,0:T(8,128)} collective-permute-done((f32[192,384]{1,0:T(8,128)}, f32[192,384]{1,0:T(8,128)}, u32[]{:S(2)}, u32[]{:S(2)}) %collective-permute-start.31) | collective-permute-done | bytes 294944 | tf_op jit(solution)/shard_map/ppermute | solution.py:164
  213.7 6.7 %collective-permute-done.32 = f32[192,384]{1,0:T(8,128)} collective-permute-done((f32[192,384]{1,0:T(8,128)}, f32[192,384]{1,0:T(8,128)}, u32[]{:S(2)}, u32[]{:S(2)}) %collective-permute-start.32) | collective-permute-done | bytes 294944 | tf_op jit(solution)/shard_map/ppermute | solution.py:164
  228.5 1.8 collective-permute-done.35
  (133 shorter events, 20.6 us)
Async XLA Ops:
  2.3 6.4 %copy-start.9 = (s32[16]{0:T(128)S(1)}, s32[16]{0:T(128)}, u32[]{:S(2)}) copy-start(s32[16]{0:T(128)} %constant.121.clone) | copy-start | bytes 196
  2.3 6.5 %copy-start.5 = (s32[32]{0:T(128)S(1)}, s32[32]{0:T(128)}, u32[]{:S(2)}) copy-start(s32[32]{0:T(128)} %param.13) | copy-start | bytes 388
  2.3 6.5 %copy-start.8 = (s32[32]{0:T(128)S(1)}, s32[32]{0:T(128)}, u32[]{:S(2)}) copy-start(s32[32]{0:T(128)} %param.12) | copy-start | bytes 388
  2.3 26.2 %collective-permute-start.1 = (f32[2112,128]{1,0:T(8,128)}, f32[2112,128]{1,0:T(8,128)}, u32[]{:S(2)}, u32[]{:S(2)}) collective-permute-start(f32[2112,128]{1,0:T(8,128)} %slice.129.t_ref), channel_id=1, source_target_pairs={{0,48},{16,0},{32,16},{48,32},{64,112},{80,64},{96,80},{112,96},{1... | collective-permute-start | bytes 3244040 | tf_op jit(solution)/shard_map/ppermute | solution.py:198
  5.6 24.7 %collective-permute-start.2 = (f32[2112,128]{1,0:T(8,128)}, f32[2112,128]{1,0:T(8,128)}, u32[]{:S(2)}, u32[]{:S(2)}) collective-permute-start(f32[2112,128]{1,0:T(8,128)} %slice.129.t_ref), channel_id=1, source_target_pairs={{0,64},{16,80},{32,96},{48,112},{64,0},{80,16},{96,32},{112,48},{1... | collective-permute-start | bytes 3244040 | tf_op jit(solution)/shard_map/ppermute | solution.py:198
  8.6 10.3 %copy-start.2 = (f32[2144,128]{1,0:T(8,128)}, f32[2144,128]{1,0:T(8,128)S(1)}, u32[]{:S(2)}) copy-start(f32[2144,128]{1,0:T(8,128)S(1)} %get-tuple-element.96.t_ref) | copy-start | bytes 3293188
  8.6 25.9 %collective-permute-start = (f32[2144,128]{1,0:T(8,128)S(1)}, f32[2144,128]{1,0:T(8,128)}, u32[]{:S(2)}, u32[]{:S(2)}) collective-permute-start(f32[2144,128]{1,0:T(8,128)S(1)} %get-tuple-element.107.t_ref), channel_id=1, source_target_pairs={{0,16},{16,32},{32,48},{48,0},{64,80},{80,96},{96,112},{112,64},{1... | collective-permute-start | bytes 3293192 | tf_op jit(solution)/shard_map/ppermute | solution.py:198
  9.0 4.7 %copy-start = (f32[8,800,512]{2,1,0:T(8,128)S(1)}, f32[8,800,512]{2,1,0:T(8,128)}, u32[]{:S(2)}) copy-start(f32[8,800,512]{2,1,0:T(8,128)} %param.9) | copy-start | bytes 39321604
  21.1 13.5 %copy-start.3 = (f32[2144,128]{1,0:T(8,128)S(1)}, f32[2144,128]{1,0:T(8,128)}, u32[]{:S(2)}) copy-start(f32[2144,128]{1,0:T(8,128)} %copy-done.2) | copy-start | bytes 3293188
  34.5 24.5 %collective-permute-start.5 = (f32[2144,128]{1,0:T(8,128)}, f32[2144,128]{1,0:T(8,128)S(1)}, u32[]{:S(2)}, u32[]{:S(2)}) collective-permute-start(f32[2144,128]{1,0:T(8,128)} %collective-permute-done.t_ref), channel_id=1, source_target_pairs={{0,64},{16,80},{32,96},{48,112},{64,0},{80,16},{96,32},{112,48},{1... | collective-permute-start | bytes 3293192 | tf_op jit(solution)/shard_map/ppermute | solution.py:198
  34.7 24.3 %collective-permute-start.4 = (f32[2144,128]{1,0:T(8,128)S(1)}, f32[2144,128]{1,0:T(8,128)S(1)}, u32[]{:S(2)}, u32[]{:S(2)}) collective-permute-start(f32[2144,128]{1,0:T(8,128)S(1)} %copy-done.3), channel_id=1, source_target_pairs={{0,48},{16,0},{32,16},{48,32},{64,112},{80,64},{96,80},{112,96},{1... | collective-permute-start | bytes 3293192 | tf_op jit(solution)/shard_map/ppermute | solution.py:198
  34.7 24.3 %collective-permute-start.3 = (f32[2112,128]{1,0:T(8,128)}, f32[2112,128]{1,0:T(8,128)S(1)}, u32[]{:S(2)}, u32[]{:S(2)}) collective-permute-start(f32[2112,128]{1,0:T(8,128)} %slice.129.t_ref), channel_id=1, source_target_pairs={{0,16},{16,32},{32,48},{48,0},{64,80},{80,96},{96,112},{112,64},{1... | collective-permute-start | bytes 3244040 | tf_op jit(solution)/shard_map/ppermute | solution.py:198
  36.2 17.6 %collective-permute-start.6 = (f32[768,128]{1,0:T(8,128)S(1)}, f32[768,128]{1,0:T(8,128)S(1)}, u32[]{:S(2)}, u32[]{:S(2)}) collective-permute-start(f32[768,128]{1,0:T(8,128)S(1)} %slice.101), channel_id=1, source_target_pairs={{0,1},{1,0},{2,3},{3,2},{4,5},{5,4},{6,7},{7,6},{8,9},{9,8},{10,11... | collective-permute-start | bytes 1179656 | tf_op jit(solution)/shard_map/ppermute | solution.py:164
  39.2 4.7 %copy-start.1 = (f32[8,800,512]{2,1,0:T(8,128)S(1)}, f32[8,800,512]{2,1,0:T(8,128)}, u32[]{:S(2)}) copy-start(f32[8,800,512]{2,1,0:T(8,128)} %param.9) | copy-start | bytes 39321604
  59.0 23.6 %collective-permute-start.7 = (f32[2144,128]{1,0:T(8,128)S(1)}, f32[2144,128]{1,0:T(8,128)S(1)}, u32[]{:S(2)}, u32[]{:S(2)}) collective-permute-start(f32[2144,128]{1,0:T(8,128)S(1)} %copy-done.3), channel_id=1, source_target_pairs={{0,16},{16,32},{32,48},{48,0},{64,80},{80,96},{96,112},{112,64},{1... | collective-permute-start | bytes 3293192 | tf_op jit(solution)/shard_map/ppermute | solution.py:198
  59.0 23.5 %collective-permute-start.8 = (f32[2144,128]{1,0:T(8,128)S(1)}, f32[2144,128]{1,0:T(8,128)S(1)}, u32[]{:S(2)}, u32[]{:S(2)}) collective-permute-start(f32[2144,128]{1,0:T(8,128)S(1)} %collective-permute-done.5.t_ref), channel_id=1, source_target_pairs={{0,48},{16,0},{32,16},{48,32},{64,112},{80,64},{96,80},{112,96},{1... | collective-permute-start | bytes 3293192 | tf_op jit(solution)/shard_map/ppermute | solution.py:198
  61.7 21.8 %collective-permute-start.9 = (f32[2144,128]{1,0:T(8,128)S(1)}, f32[2144,128]{1,0:T(8,128)S(1)}, u32[]{:S(2)}, u32[]{:S(2)}) collective-permute-start(f32[2144,128]{1,0:T(8,128)S(1)} %copy-done.3), channel_id=1, source_target_pairs={{0,64},{16,80},{32,96},{48,112},{64,0},{80,16},{96,32},{112,48},{1... | collective-permute-start | bytes 3293192 | tf_op jit(solution)/shard_map/ppermute | solution.py:198
  63.0 7.2 %collective-permute-start.10 = (f32[384,128]{1,0:T(8,128)S(1)}, f32[384,128]{1,0:T(8,128)S(1)}, u32[]{:S(2)}, u32[]{:S(2)}) collective-permute-start(f32[384,128]{1,0:T(8,128)S(1)} %slice.103), channel_id=1, source_target_pairs={{0,4},{1,5},{2,6},{3,7},{4,0},{5,1},{6,2},{7,3},{8,12},{9,13},{10,... | collective-permute-start | bytes 589832 | tf_op jit(solution)/shard_map/ppermute | solution.py:164
  83.5 22.6 %collective-permute-start.11 = (f32[2144,128]{1,0:T(8,128)S(1)}, f32[2144,128]{1,0:T(8,128)S(1)}, u32[]{:S(2)}, u32[]{:S(2)}) collective-permute-start(f32[2144,128]{1,0:T(8,128)S(1)} %collective-permute-done.9.t_ref), channel_id=1, source_target_pairs={{0,16},{16,32},{32,48},{48,0},{64,80},{80,96},{96,112},{112,64},{1... | collective-permute-start | bytes 3293192 | tf_op jit(solution)/shard_map/ppermute | solution.py:198
  83.5 22.6 %collective-permute-start.12 = (f32[2144,128]{1,0:T(8,128)S(1)}, f32[2144,128]{1,0:T(8,128)S(1)}, u32[]{:S(2)}, u32[]{:S(2)}) collective-permute-start(f32[2144,128]{1,0:T(8,128)S(1)} %get-tuple-element.107.t_ref), channel_id=1, source_target_pairs={{0,48},{16,0},{32,16},{48,32},{64,112},{80,64},{96,80},{112,96},{1... | collective-permute-start | bytes 3293192 | tf_op jit(solution)/shard_map/ppermute | solution.py:198
  86.1 20.0 %collective-permute-start.13 = (f32[2112,128]{1,0:T(8,128)S(1)}, f32[2112,128]{1,0:T(8,128)S(1)}, u32[]{:S(2)}, u32[]{:S(2)}) collective-permute-start(f32[2112,128]{1,0:T(8,128)S(1)} %collective-permute-done.3.t_ref), channel_id=1, source_target_pairs={{0,64},{16,80},{32,96},{48,112},{64,0},{80,16},{96,32},{112,48},{1... | collective-permute-start | bytes 3244040 | tf_op jit(solution)/shard_map/ppermute | solution.py:198
  89.0 31.4 %slice-start = ((s8[13107200]{0:T(1024)(128)(4,1)}), s8[4194304]{0:T(1024)(128)(4,1)S(1)}, s32[]{:S(2)}) async-start(s8[13107200]{0:T(1024)(128)(4,1)} %bitcast.26), calls=%async_computation | async-start | bytes 8388608
  89.0 31.4 %slice-start.1 = ((s8[13107200]{0:T(1024)(128)(4,1)}), s8[4194304]{0:T(1024)(128)(4,1)S(1)}, s32[]{:S(2)}) async-start(s8[13107200]{0:T(1024)(128)(4,1)} %bitcast.26), calls=%async_computation.1 | async-start | bytes 8388608
  90.7 29.8 %slice-start.2 = ((s8[13107200]{0:T(1024)(128)(4,1)}), s8[4194304]{0:T(1024)(128)(4,1)S(1)}, s32[]{:S(2)}) async-start(s8[13107200]{0:T(1024)(128)(4,1)} %bitcast.26), calls=%async_computation.2 | async-start | bytes 8388608
  90.7 29.8 %slice-start.3 = ((s8[13107200]{0:T(1024)(128)(4,1)}), s8[524288]{0:T(1024)(128)(4,1)S(1)}, s32[]{:S(2)}) async-start(s8[13107200]{0:T(1024)(128)(4,1)} %bitcast.26), calls=%async_computation.3 | async-start | bytes 1048576
  92.3 5.9 %collective-permute-start.14 = (f32[192,128]{1,0:T(8,128)S(1)}, f32[192,128]{1,0:T(8,128)S(1)}, u32[]{:S(2)}, u32[]{:S(2)}) collective-permute-start(f32[192,128]{1,0:T(8,128)S(1)} %slice.105), channel_id=1, source_target_pairs={{0,8},{1,9},{2,10},{3,11},{4,12},{5,13},{6,14},{7,15},{8,0},{9,1},... | collective-permute-start | bytes 294920 | tf_op jit(solution)/shard_map/ppermute | solution.py:164
  106.1 22.2 %collective-permute-start.15 = (f32[2144,128]{1,0:T(8,128)}, f32[2144,128]{1,0:T(8,128)S(1)}, u32[]{:S(2)}, u32[]{:S(2)}) collective-permute-start(f32[2144,128]{1,0:T(8,128)} %collective-permute-done.t_ref), channel_id=1, source_target_pairs={{0,16},{16,32},{32,48},{48,0},{64,80},{80,96},{96,112},{112,64},{1... | collective-permute-start | bytes 3293192 | tf_op jit(solution)/shard_map/ppermute | solution.py:198
  106.1 22.7 %collective-permute-start.17 = (f32[2144,128]{1,0:T(8,128)S(1)}, f32[2144,128]{1,0:T(8,128)S(1)}, u32[]{:S(2)}, u32[]{:S(2)}) collective-permute-start(f32[2144,128]{1,0:T(8,128)S(1)} %collective-permute-done.12.t_ref), channel_id=1, source_target_pairs={{0,64},{16,80},{32,96},{48,112},{64,0},{80,16},{96,32},{112,48},{1... | collective-permute-start | bytes 3293192 | tf_op jit(solution)/shard_map/ppermute | solution.py:198
  107.5 20.8 %collective-permute-start.16 = (f32[2112,128]{1,0:T(8,128)}, f32[2112,128]{1,0:T(8,128)S(1)}, u32[]{:S(2)}, u32[]{:S(2)}) collective-permute-start(f32[2112,128]{1,0:T(8,128)} %collective-permute-done.1.t_ref), channel_id=1, source_target_pairs={{0,48},{16,0},{32,16},{48,32},{64,112},{80,64},{96,80},{112,96},{1... | collective-permute-start | bytes 3244040 | tf_op jit(solution)/shard_map/ppermute | solution.py:198
  110.1 18.0 %collective-permute-start.18 = (f32[768,256]{1,0:T(8,128)S(1)}, f32[768,256]{1,0:T(8,128)S(1)}, u32[]{:S(2)}, u32[]{:S(2)}) collective-permute-start(f32[768,256]{1,0:T(8,128)S(1)} %slice.107), channel_id=1, source_target_pairs={{0,1},{1,0},{2,3},{3,2},{4,5},{5,4},{6,7},{7,6},{8,9},{9,8},{10,11... | collective-permute-start | bytes 2359304 | tf_op jit(solution)/shard_map/ppermute | solution.py:164
  128.8 27.1 %collective-permute-start.19 = (f32[2144,128]{1,0:T(8,128)S(1)}, f32[2144,128]{1,0:T(8,128)S(1)}, u32[]{:S(2)}, u32[]{:S(2)}) collective-permute-start(f32[2144,128]{1,0:T(8,128)S(1)} %collective-permute-done.7.t_ref), channel_id=1, source_target_pairs={{0,16},{16,32},{32,48},{48,0},{64,80},{80,96},{96,112},{112,64},{1... | collective-permute-start | bytes 3293192 | tf_op jit(solution)/shard_map/ppermute | solution.py:198
  129.2 26.7 %collective-permute-start.21 = (f32[2144,128]{1,0:T(8,128)S(1)}, f32[2144,128]{1,0:T(8,128)S(1)}, u32[]{:S(2)}, u32[]{:S(2)}) collective-permute-start(f32[2144,128]{1,0:T(8,128)S(1)} %collective-permute-done.4.t_ref), channel_id=1, source_target_pairs={{0,64},{16,80},{32,96},{48,112},{64,0},{80,16},{96,32},{112,48},{1... | collective-permute-start | bytes 3293192 | tf_op jit(solution)/shard_map/ppermute | solution.py:198
  130.4 25.5 %collective-permute-start.20 = (f32[2112,128]{1,0:T(8,128)}, f32[2112,128]{1,0:T(8,128)S(1)}, u32[]{:S(2)}, u32[]{:S(2)}) collective-permute-start(f32[2112,128]{1,0:T(8,128)} %collective-permute-done.2.t_ref), channel_id=1, source_target_pairs={{0,48},{16,0},{32,16},{48,32},{64,112},{80,64},{96,80},{112,96},{1... | collective-permute-start | bytes 3244040 | tf_op jit(solution)/shard_map/ppermute | solution.py:198
  132.8 22.9 %collective-permute-start.23 = (f32[768,256]{1,0:T(8,128)S(1)}, f32[768,256]{1,0:T(8,128)S(1)}, u32[]{:S(2)}, u32[]{:S(2)}) collective-permute-start(f32[768,256]{1,0:T(8,128)S(1)} %slice.111), channel_id=1, source_target_pairs={{0,1},{1,0},{2,3},{3,2},{4,5},{5,4},{6,7},{7,6},{8,9},{9,8},{10,11... | collective-permute-start | bytes 2359304 | tf_op jit(solution)/shard_map/ppermute | solution.py:164
  144.6 11.1 %collective-permute-start.22 = (f32[384,256]{1,0:T(8,128)S(1)}, f32[384,256]{1,0:T(8,128)S(1)}, u32[]{:S(2)}, u32[]{:S(2)}) collective-permute-start(f32[384,256]{1,0:T(8,128)S(1)} %slice.109), channel_id=1, source_target_pairs={{0,4},{1,5},{2,6},{3,7},{4,0},{5,1},{6,2},{7,3},{8,12},{9,13},{10,... | collective-permute-start | bytes 1179656 | tf_op jit(solution)/shard_map/ppermute | solution.py:164
  155.9 21.7 %collective-permute-start.25 = (f32[2144,128]{1,0:T(8,128)S(1)}, f32[2144,128]{1,0:T(8,128)S(1)}, u32[]{:S(2)}, u32[]{:S(2)}) collective-permute-start(f32[2144,128]{1,0:T(8,128)S(1)} %collective-permute-done.21.t_ref), channel_id=1, source_target_pairs={{0,48},{16,0},{32,16},{48,32},{64,112},{80,64},{96,80},{112,96},{1... | collective-permute-start | bytes 3293192 | tf_op jit(solution)/shard_map/ppermute | solution.py:198
  156.0 21.6 %collective-permute-start.26 = (f32[2144,128]{1,0:T(8,128)S(1)}, f32[2144,128]{1,0:T(8,128)S(1)}, u32[]{:S(2)}, u32[]{:S(2)}) collective-permute-start(f32[2144,128]{1,0:T(8,128)S(1)} %collective-permute-done.15.t_ref), channel_id=1, source_target_pairs={{0,64},{16,80},{32,96},{48,112},{64,0},{80,16},{96,32},{112,48},{1... | collective-permute-start | bytes 3293192 | tf_op jit(solution)/shard_map/ppermute | solution.py:198
  156.1 19.1 %collective-permute-start.24 = (f32[2112,128]{1,0:T(8,128)S(1)}, f32[2112,128]{1,0:T(8,128)S(1)}, u32[]{:S(2)}, u32[]{:S(2)}) collective-permute-start(f32[2112,128]{1,0:T(8,128)S(1)} %collective-permute-done.13.t_ref), channel_id=1, source_target_pairs={{0,16},{16,32},{32,48},{48,0},{64,80},{80,96},{96,112},{112,64},{1... | collective-permute-start | bytes 3244040 | tf_op jit(solution)/shard_map/ppermute | solution.py:198
  161.3 12.3 %collective-permute-start.28 = (f32[384,256]{1,0:T(8,128)S(1)}, f32[384,256]{1,0:T(8,128)S(1)}, u32[]{:S(2)}, u32[]{:S(2)}) collective-permute-start(f32[384,256]{1,0:T(8,128)S(1)} %slice.115), channel_id=1, source_target_pairs={{0,4},{1,5},{2,6},{3,7},{4,0},{5,1},{6,2},{7,3},{8,12},{9,13},{10,... | collective-permute-start | bytes 1179656 | tf_op jit(solution)/shard_map/ppermute | solution.py:164
  163.0 10.6 %collective-permute-start.27 = (f32[192,256]{1,0:T(8,128)S(1)}, f32[192,256]{1,0:T(8,128)S(1)}, u32[]{:S(2)}, u32[]{:S(2)}) collective-permute-start(f32[192,256]{1,0:T(8,128)S(1)} %slice.113), channel_id=1, source_target_pairs={{0,8},{1,9},{2,10},{3,11},{4,12},{5,13},{6,14},{7,15},{8,0},{9,1},... | collective-permute-start | bytes 589832 | tf_op jit(solution)/shard_map/ppermute | solution.py:164
  185.3 14.8 %collective-permute-start.29 = (f32[768,384]{1,0:T(8,128)S(1)}, f32[768,384]{1,0:T(8,128)S(1)}, u32[]{:S(2)}, u32[]{:S(2)}) collective-permute-start(f32[768,384]{1,0:T(8,128)S(1)} %slice.117), channel_id=1, source_target_pairs={{0,1},{1,0},{2,3},{3,2},{4,5},{5,4},{6,7},{7,6},{8,9},{9,8},{10,11... | collective-permute-start | bytes 3538952 | tf_op jit(solution)/shard_map/ppermute | solution.py:164
  191.5 8.7 %collective-permute-start.30 = (f32[192,256]{1,0:T(8,128)S(1)}, f32[192,256]{1,0:T(8,128)S(1)}, u32[]{:S(2)}, u32[]{:S(2)}) collective-permute-start(f32[192,256]{1,0:T(8,128)S(1)} %slice.119), channel_id=1, source_target_pairs={{0,8},{1,9},{2,10},{3,11},{4,12},{5,13},{6,14},{7,15},{8,0},{9,1},... | collective-permute-start | bytes 589832 | tf_op jit(solution)/shard_map/ppermute | solution.py:164
  200.4 7.4 %collective-permute-start.34 = (f32[96,384]{1,0:T(8,128)S(1)}, f32[96,384]{1,0:T(8,128)S(1)}, u32[]{:S(2)}, u32[]{:S(2)}) collective-permute-start(f32[96,384]{1,0:T(8,128)S(1)} %slice.133), channel_id=1, source_target_pairs={{0,2},{1,3},{2,0},{3,1},{4,6},{5,7},{6,4},{7,5},{8,10},{9,11},{10,... | collective-permute-start | bytes 442376 | tf_op jit(solution)/shard_map/ppermute | solution.py:164
  204.2 9.5 %collective-permute-start.31 = (f32[192,384]{1,0:T(8,128)}, f32[192,384]{1,0:T(8,128)}, u32[]{:S(2)}, u32[]{:S(2)}) collective-permute-start(f32[192,384]{1,0:T(8,128)} %get-tuple-element.175), channel_id=1, source_target_pairs={{0,8},{1,9},{2,10},{3,11},{4,12},{5,13},{6,14},{7,15},{8,0},{9,1},... | collective-permute-start | bytes 884744 | tf_op jit(solution)/shard_map/ppermute | solution.py:164
  207.0 13.4 %collective-permute-start.32 = (f32[192,384]{1,0:T(8,128)}, f32[192,384]{1,0:T(8,128)}, u32[]{:S(2)}, u32[]{:S(2)}) collective-permute-start(f32[192,384]{1,0:T(8,128)} %get-tuple-element.177), channel_id=1, source_target_pairs={{0,4},{1,5},{2,6},{3,7},{4,0},{5,1},{6,2},{7,3},{8,12},{9,13},{10,... | collective-permute-start | bytes 884744 | tf_op jit(solution)/shard_map/ppermute | solution.py:164
  207.8 13.4 %collective-permute-start.33 = (f32[192,384]{1,0:T(8,128)}, f32[192,384]{1,0:T(8,128)}, u32[]{:S(2)}, u32[]{:S(2)}) collective-permute-start(f32[192,384]{1,0:T(8,128)} %get-tuple-element.176), channel_id=1, source_target_pairs={{0,12},{1,13},{2,14},{3,15},{4,8},{5,9},{6,10},{7,11},{8,4},{9,5},... | collective-permute-start | bytes 884744 | tf_op jit(solution)/shard_map/ppermute | solution.py:164
  207.8 14.9 %copy-start.4 = (s32[8]{0:T(128)S(1)}, s32[8]{0:T(128)}, u32[]{:S(2)}) copy-start(s32[8]{0:T(128)} %constant.122.clone) | copy-start | bytes 100
  222.4 6.0 %copy-start.7 = (f32[512]{0:T(512)S(1)}, f32[512]{0:T(512)}, u32[]{:S(2)}) copy-start(f32[512]{0:T(512)} %param.10) | copy-start | bytes 6148
  222.5 7.8 %collective-permute-start.35 = (f32[96,640]{1,0:T(8,128)S(1)}, f32[96,640]{1,0:T(8,128)S(1)}, u32[]{:S(2)}, u32[]{:S(2)}) collective-permute-start(f32[96,640]{1,0:T(8,128)S(1)} %slice.135), channel_id=1, source_target_pairs={{0,2},{1,3},{2,0},{3,1},{4,6},{5,7},{6,4},{7,5},{8,10},{9,11},{10,... | collective-permute-start | bytes 737288 | tf_op jit(solution)/shard_map/ppermute | solution.py:164
  230.4 0.7 copy-start.6
where the time goes:
time: 233 us; the launch traced here: 232 us
  starting transfers between devices  77.3 us (33%)
  waiting for transfers between devices  69.8 us (30%)
  Pallas kernels  58.5 us (25%)
  local copies, waits for them, and re-layouts  16.1 us (7%)
  between operations  5.79 us (2%)
  other arithmetic  4.53 us (2%)
    ppermute x15, starting transfers between devices, swap(): return lax.ppermute(part, 'vslab', [(i, i ^ bits) for i in range(owners)])  53.5 us
    pallas_call x24, Pallas kernels, product(): pl.pallas_call(product_kernel, grid=(steps,), in_specs=[pl.BlockSpec((til...  48.3 us
    ppermute x21, waiting for transfers between devices, on_device(): lax.ppermute(held[p, offset], 'blk', link_pairs(STEPS[link]))  42.1 us
    ppermute x15, waiting for transfers between devices, swap(): return lax.ppermute(part, 'vslab', [(i, i ^ bits) for i in range(owners)])  27.6 us
    ppermute x21, starting transfers between devices, on_device(): lax.ppermute(held[p, offset], 'blk', link_pairs(STEPS[link]))  23.8 us
    pallas_call x5, Pallas kernels, pack(): pl.pallas_call(pack_kernel, grid=(4,), in_specs=[pl.BlockSpec((tile, hot....  10.1 us
    unnamed x30, local copies, waits for them, and re-layouts  10.1 us
  transfers between devices with their start and end apart: 36, of which 17 were waited for; matrix products, arithmetic and copies ran while one was open for 2% of the time, Pallas kernels for 22%

commit v1 on v0

--- a/solution.py
+++ b/solution.py
@@ -213,16 +213,19 @@
         multiply(p, offset)
         count[offset] = count.get(offset, 0) + 1
     start_batches()
-    own, first, second, third, last = parts
-    last = jnp.concatenate([third, step("pack", last)], axis=1)
-    last, second, own, first = lax.optimization_barrier((last, second, own, first))
+    early, (second, third, last) = jnp.concatenate(parts[:2], axis=1), parts[2:]
+    last = step("pack", last)
+    third = step("core", third)
+    last, third, second, early = lax.optimization_barrier((last, third, second, early))
     last = step("core", last)
+    third = sum_z(third)
+    last, third, second, early = lax.optimization_barrier((last, third, second, early))
+    last = sum_z(last)
     second = step("far", second)
-    last, second, own, first = lax.optimization_barrier((last, second, own, first))
-    last = sum_z(last)
-    settled = step("y", jnp.concatenate([own, first], axis=1))
-    last, second, settled = lax.optimization_barrier((last, second, settled))
-    parts = [settled, step("y", jnp.concatenate([second, last], axis=1))]
+    early = step("y", jnp.concatenate([early, third], axis=1))
+    last, second, early = lax.optimization_barrier((last, second, early))
+    parts = [early, step("y", jnp.concatenate([second, last], axis=1))]
+    order = order[:3] + order[5:7] + order[3:5] + order[7:]
 
     me = lax.axis_index("blk")
     my_x, my_y = me % NX, me // NX

time: 233 us -> 230 us (0.987)
  waiting for transfers between devices: 69.8 us -> 61.8 us
  starting transfers between devices: 77.3 us -> 82.5 us
    ppermute x15 -> x19, waiting for transfers between devices: 27.6 us -> 19.6 us  [swap(): return lax.ppermute(part, 'vslab', [(i, i ^ bits) for i in range(owners)])]
    ppermute x15 -> x19, starting transfers between devices: 53.5 us -> 58.7 us  [swap(): return lax.ppermute(part, 'vslab', [(i, i ^ bits) for i in range(owners)])]
  transfers between devices with their start and end apart: 36 -> 40, of which waited for: 17 -> 15; matrix products, arithmetic and copies ran while one was open for 2% -> 2% of each run, Pallas kernels for 22% -> 26%
where the time goes in v1:
time: 230 us; the launch traced here: 227 us
  starting transfers between devices  82.5 us (36%)
  waiting for transfers between devices  61.8 us (27%)
  Pallas kernels  58.4 us (25%)
  local copies, waits for them, and re-layouts  15.3 us (7%)
  between operations  6.15 us (3%)
  other arithmetic  3.33 us (1%)
    ppermute x19, starting transfers between devices, swap(): return lax.ppermute(part, 'vslab', [(i, i ^ bits) for i in range(owners)])  58.7 us
    pallas_call x24, Pallas kernels, product(): pl.pallas_call(product_kernel, grid=(steps,), in_specs=[pl.BlockSpec((til...  48.3 us
    ppermute x21, waiting for transfers between devices, on_device(): lax.ppermute(held[p, offset], 'blk', link_pairs(STEPS[link]))  42.1 us
    ppermute x21, starting transfers between devices, on_device(): lax.ppermute(held[p, offset], 'blk', link_pairs(STEPS[link]))  23.8 us
    ppermute x19, waiting for transfers between devices, swap(): return lax.ppermute(part, 'vslab', [(i, i ^ bits) for i in range(owners)])  19.6 us
    pallas_call x5, Pallas kernels, pack(): pl.pallas_call(pack_kernel, grid=(4,), in_specs=[pl.BlockSpec((tile, hot....  10.1 us
    unnamed x30, local copies, waits for them, and re-layouts  10.1 us
  transfers between devices with their start and end apart: 40, of which 15 were waited for; matrix products, arithmetic and copies ran while one was open for 2% of the time, Pallas kernels for 26%

profile of v1, /device:TPU:1, one launch (start us, length us, event | category | flops | bytes accessed | tf_op | source)
XLA Modules:
  0.0 227.4 jit_solution(3372054131248048892)
XLA Ops:
  0.0 2.3 %slice.153.t_ref = f32[2112,128]{1,0:T(8,128)} slice(f32[6400,128]{1,0:T(8,128)} %bitcast.40), slice={[0:2112], [0:128]} | slice | bytes 2162688 | tf_op jit(solution)/shard_map/slice | solution.py:141
  2.3 3.3 %collective-permute-start.1 = (f32[2112,128]{1,0:T(8,128)}, f32[2112,128]{1,0:T(8,128)}, u32[]{:S(2)}, u32[]{:S(2)}) collective-permute-start(f32[2112,128]{1,0:T(8,128)} %slice.153.t_ref), channel_id=1, source_target_pairs={{0,48},{16,0},{32,16},{48,32},{64,112},{80,64},{96,80},{112,96},{1... | collective-permute-start | bytes 3244040 | tf_op jit(solution)/shard_map/ppermute | solution.py:198
  6.9 1.7 fusion.19
  9.0 4.7 %copy-done = f32[8,800,512]{2,1,0:T(8,128)S(1)} copy-done((f32[8,800,512]{2,1,0:T(8,128)S(1)}, f32[8,800,512]{2,1,0:T(8,128)}, u32[]{:S(2)}) %copy-start) | copy-done | bytes 13107224
  13.7 1.6 product.25
  15.3 3.6 %product.24 = f32[128,512]{1,0:T(8,128)S(1)} custom-call(f32[2112,128]{1,0:T(8,128)} %slice.153.t_ref, f32[6400,512]{1,0:T(8,128)S(1)} %bitcast.15), custom_call_target="tpu_custom_call" | custom-call | flops 1 | bytes 1 | tf_op jit(solution)/shard_map/product/pallas_call | solution.py:89
  18.9 1.6 product.26
  21.1 1.9 pack.5
  23.1 5.4 %collective-permute-done.1.t_ref = f32[2112,128]{1,0:T(8,128)} collective-permute-done((f32[2112,128]{1,0:T(8,128)}, f32[2112,128]{1,0:T(8,128)}, u32[]{:S(2)}, u32[]{:S(2)}) %collective-permute-start.1) | collective-permute-done | bytes 1081376 | tf_op jit(solution)/shard_map/ppermute | solution.py:198
  28.4 1.9 collective-permute-done.2.t_ref
  30.3 4.1 %collective-permute-done.t_ref = f32[2144,128]{1,0:T(8,128)} collective-permute-done((f32[2144,128]{1,0:T(8,128)S(1)}, f32[2144,128]{1,0:T(8,128)}, u32[]{:S(2)}, u32[]{:S(2)}) %collective-permute-start) | collective-permute-done | bytes 1097760 | tf_op jit(solution)/shard_map/ppermute | solution.py:198
  36.1 3.1 %collective-permute-start.6 = (f32[768,128]{1,0:T(8,128)S(1)}, f32[768,128]{1,0:T(8,128)S(1)}, u32[]{:S(2)}, u32[]{:S(2)}) collective-permute-start(f32[768,128]{1,0:T(8,128)S(1)} %slice.119), channel_id=1, source_target_pairs={{0,1},{1,0},{2,3},{3,2},{4,5},{5,4},{6,7},{7,6},{8,9},{9,8},{10,11... | collective-permute-start | bytes 1179656 | tf_op jit(solution)/shard_map/ppermute | solution.py:164
  39.2 4.7 %copy-done.1 = f32[8,800,512]{2,1,0:T(8,128)S(1)} copy-done((f32[8,800,512]{2,1,0:T(8,128)S(1)}, f32[8,800,512]{2,1,0:T(8,128)}, u32[]{:S(2)}) %copy-start.1) | copy-done | bytes 13107224
  43.9 2.6 %product.27 = f32[128,512]{1,0:T(8,128)S(1)} custom-call(f32[2144,128]{1,0:T(8,128)} %collective-permute-done.t_ref, f32[6400,512]{1,0:T(8,128)S(1)} %bitcast.17), custom_call_target="tpu_custom_call" | custom-call | flops 1 | bytes 1 | tf_op jit(solution)/shard_map/product/pallas_call | solution.py:89
  46.6 3.6 %product.28 = f32[128,512]{1,0:T(8,128)S(1)} custom-call(f32[2112,128]{1,0:T(8,128)} %collective-permute-done.1.t_ref, f32[6400,512]{1,0:T(8,128)S(1)} %bitcast.18), custom_call_target="tpu_custom_call" | custom-call | flops 1 | bytes 1 | tf_op jit(solution)/shard_map/product/pallas_call | solution.py:89
  50.1 3.6 %product.29 = f32[128,512]{1,0:T(8,128)S(1)} custom-call(f32[2112,128]{1,0:T(8,128)} %collective-permute-done.2.t_ref, f32[6400,512]{1,0:T(8,128)S(1)} %bitcast.19), custom_call_target="tpu_custom_call" | custom-call | flops 1 | bytes 1 | tf_op jit(solution)/shard_map/product/pallas_call | solution.py:89
  53.8 5.2 %collective-permute-done.3.t_ref = f32[2112,128]{1,0:T(8,128)S(1)} collective-permute-done((f32[2112,128]{1,0:T(8,128)}, f32[2112,128]{1,0:T(8,128)S(1)}, u32[]{:S(2)}, u32[]{:S(2)}) %collective-permute-start.3) | collective-permute-done | bytes 1081376 | tf_op jit(solution)/shard_map/ppermute | solution.py:198
  59.0 2.7 %collective-permute-start.8 = (f32[2144,128]{1,0:T(8,128)S(1)}, f32[2144,128]{1,0:T(8,128)S(1)}, u32[]{:S(2)}, u32[]{:S(2)}) collective-permute-start(f32[2144,128]{1,0:T(8,128)S(1)} %collective-permute-done.5.t_ref), channel_id=1, source_target_pairs={{0,48},{16,0},{32,16},{48,32},{64,112},{80,64},{96,80},{112,96},{1... | collective-permute-start | bytes 3293192 | tf_op jit(solution)/shard_map/ppermute | solution.py:198
  63.0 1.7 collective-permute-start.10
  64.7 1.6 product.32
  66.3 1.6 product.31
  68.0 2.2 product.30
  70.3 12.3 %collective-permute-done.7.t_ref = f32[2144,128]{1,0:T(8,128)S(1)} collective-permute-done((f32[2144,128]{1,0:T(8,128)S(1)}, f32[2144,128]{1,0:T(8,128)S(1)}, u32[]{:S(2)}, u32[]{:S(2)}) %collective-permute-start.7) | collective-permute-done | bytes 1097760 | tf_op jit(solution)/shard_map/ppermute | solution.py:198
  83.5 2.7 %collective-permute-start.12 = (f32[2144,128]{1,0:T(8,128)S(1)}, f32[2144,128]{1,0:T(8,128)S(1)}, u32[]{:S(2)}, u32[]{:S(2)}) collective-permute-start(f32[2144,128]{1,0:T(8,128)S(1)} %get-tuple-element.107.t_ref), channel_id=1, source_target_pairs={{0,48},{16,0},{32,16},{48,32},{64,112},{80,64},{96,80},{112,96},{1... | collective-permute-start | bytes 3293192 | tf_op jit(solution)/shard_map/ppermute | solution.py:198
  87.5 1.6 product.35
  89.1 1.6 product.33
  90.7 1.6 product.34
  92.3 3.6 %collective-permute-start.14 = (f32[192,128]{1,0:T(8,128)S(1)}, f32[192,128]{1,0:T(8,128)S(1)}, u32[]{:S(2)}, u32[]{:S(2)}) collective-permute-start(f32[192,128]{1,0:T(8,128)S(1)} %slice.123), channel_id=1, source_target_pairs={{0,8},{1,9},{2,10},{3,11},{4,12},{5,13},{6,14},{7,15},{8,0},{9,1},... | collective-permute-start | bytes 294920 | tf_op jit(solution)/shard_map/ppermute | solution.py:164
  96.1 2.1 pack.6
  98.2 7.8 %collective-permute-done.13.t_ref = f32[2112,128]{1,0:T(8,128)S(1)} collective-permute-done((f32[2112,128]{1,0:T(8,128)S(1)}, f32[2112,128]{1,0:T(8,128)S(1)}, u32[]{:S(2)}, u32[]{:S(2)}) %collective-permute-start.13) | collective-permute-done | bytes 1081376 | tf_op jit(solution)/shard_map/ppermute | solution.py:198
  107.5 2.6 %collective-permute-start.16 = (f32[2112,128]{1,0:T(8,128)}, f32[2112,128]{1,0:T(8,128)S(1)}, u32[]{:S(2)}, u32[]{:S(2)}) collective-permute-start(f32[2112,128]{1,0:T(8,128)} %collective-permute-done.1.t_ref), channel_id=1, source_target_pairs={{0,48},{16,0},{32,16},{48,32},{64,112},{80,64},{96,80},{112,96},{1... | collective-permute-start | bytes 3244040 | tf_op jit(solution)/shard_map/ppermute | solution.py:198
  110.1 10.3 %collective-permute-start.18 = (f32[768,256]{1,0:T(8,128)S(1)}, f32[768,256]{1,0:T(8,128)S(1)}, u32[]{:S(2)}, u32[]{:S(2)}) collective-permute-start(f32[768,256]{1,0:T(8,128)S(1)} %slice.125), channel_id=1, source_target_pairs={{0,1},{1,0},{2,3},{3,2},{4,5},{5,4},{6,7},{7,6},{8,9},{9,8},{10,11... | collective-permute-start | bytes 2359304 | tf_op jit(solution)/shard_map/ppermute | solution.py:164
  120.4 1.6 product.36
  122.0 1.6 product.37
  123.6 2.2 product.38
  126.0 2.1 pack.7
  130.4 2.4 %collective-permute-start.20 = (f32[2112,128]{1,0:T(8,128)}, f32[2112,128]{1,0:T(8,128)S(1)}, u32[]{:S(2)}, u32[]{:S(2)}) collective-permute-start(f32[2112,128]{1,0:T(8,128)} %collective-permute-done.2.t_ref), channel_id=1, source_target_pairs={{0,48},{16,0},{32,16},{48,32},{64,112},{80,64},{96,80},{112,96},{1... | collective-permute-start | bytes 3244040 | tf_op jit(solution)/shard_map/ppermute | solution.py:198
  132.8 11.8 %collective-permute-start.23 = (f32[768,256]{1,0:T(8,128)S(1)}, f32[768,256]{1,0:T(8,128)S(1)}, u32[]{:S(2)}, u32[]{:S(2)}) collective-permute-start(f32[768,256]{1,0:T(8,128)S(1)} %slice.129), channel_id=1, source_target_pairs={{0,1},{1,0},{2,3},{3,2},{4,5},{5,4},{6,7},{7,6},{8,9},{9,8},{10,11... | collective-permute-start | bytes 2359304 | tf_op jit(solution)/shard_map/ppermute | solution.py:164
  144.6 1.7 collective-permute-start.22
  146.3 1.6 product.39
  147.9 2.2 product.40
  150.1 1.6 product.41
  151.8 3.9 %collective-permute-done.22 = f32[384,256]{1,0:T(8,128)S(1)} collective-permute-done((f32[384,256]{1,0:T(8,128)S(1)}, f32[384,256]{1,0:T(8,128)S(1)}, u32[]{:S(2)}, u32[]{:S(2)}) %collective-permute-start.22) | collective-permute-done | bytes 393248 | tf_op jit(solution)/shard_map/ppermute | solution.py:164
  157.5 1.6 product.44
  159.1 2.2 product.43
  161.3 1.6 collective-permute-start.28
  163.0 3.4 %collective-permute-start.27 = (f32[192,256]{1,0:T(8,128)S(1)}, f32[192,256]{1,0:T(8,128)S(1)}, u32[]{:S(2)}, u32[]{:S(2)}) collective-permute-start(f32[192,256]{1,0:T(8,128)S(1)} %slice.131), channel_id=1, source_target_pairs={{0,8},{1,9},{2,10},{3,11},{4,12},{5,13},{6,14},{7,15},{8,0},{9,1},... | collective-permute-start | bytes 589832 | tf_op jit(solution)/shard_map/ppermute | solution.py:164
  166.4 1.6 product.42
  168.1 2.1 pack.8
  170.2 3.3 %collective-permute-done.27 = f32[192,256]{1,0:T(8,128)S(1)} collective-permute-done((f32[192,256]{1,0:T(8,128)S(1)}, f32[192,256]{1,0:T(8,128)S(1)}, u32[]{:S(2)}, u32[]{:S(2)}) %collective-permute-start.27) | collective-permute-done | bytes 196640 | tf_op jit(solution)/shard_map/ppermute | solution.py:164
  175.2 2.4 %collective-permute-done.25.t_ref = f32[2144,128]{1,0:T(8,128)S(1)} collective-permute-done((f32[2144,128]{1,0:T(8,128)S(1)}, f32[2144,128]{1,0:T(8,128)S(1)}, u32[]{:S(2)}, u32[]{:S(2)}) %collective-permute-start.25) | collective-permute-done | bytes 1097760 | tf_op jit(solution)/shard_map/ppermute | solution.py:198
  177.7 6.1 %collective-permute-start.29 = (f32[768,256]{1,0:T(8,128)S(1)}, f32[768,256]{1,0:T(8,128)S(1)}, u32[]{:S(2)}, u32[]{:S(2)}) collective-permute-start(f32[768,256]{1,0:T(8,128)S(1)} %slice.135), channel_id=1, source_target_pairs={{0,1},{1,0},{2,3},{3,2},{4,5},{5,4},{6,7},{7,6},{8,9},{9,8},{10,11... | collective-permute-start | bytes 2359304 | tf_op jit(solution)/shard_map/ppermute | solution.py:164
  183.8 2.2 product.45
  185.9 1.6 product.46
  187.6 1.6 product.47
  189.2 1.9 pack.9
  191.4 3.4 %collective-permute-start.31 = (f32[192,256]{1,0:T(8,128)S(1)}, f32[192,256]{1,0:T(8,128)S(1)}, u32[]{:S(2)}, u32[]{:S(2)}) collective-permute-start(f32[192,256]{1,0:T(8,128)S(1)} %get-tuple-element.175), channel_id=1, source_target_pairs={{0,8},{1,9},{2,10},{3,11},{4,12},{5,13},{6,14},{7,15},{8,0},{9,1},... | collective-permute-start | bytes 589832 | tf_op jit(solution)/shard_map/ppermute | solution.py:164
  196.2 3.8 %collective-permute-done.31 = f32[192,256]{1,0:T(8,128)S(1)} collective-permute-done((f32[192,256]{1,0:T(8,128)S(1)}, f32[192,256]{1,0:T(8,128)S(1)}, u32[]{:S(2)}, u32[]{:S(2)}) %collective-permute-start.31) | collective-permute-done | bytes 196640 | tf_op jit(solution)/shard_map/ppermute | solution.py:164
  200.0 4.8 %collective-permute-done.32 = f32[192,256]{1,0:T(8,128)S(1)} collective-permute-done((f32[192,256]{1,0:T(8,128)S(1)}, f32[192,256]{1,0:T(8,128)S(1)}, u32[]{:S(2)}, u32[]{:S(2)}) %collective-permute-start.32) | collective-permute-done | bytes 196640 | tf_op jit(solution)/shard_map/ppermute | solution.py:164
  205.0 2.6 %collective-permute-start.34 = (f32[192,128]{1,0:T(8,128)S(1)}, f32[192,128]{1,0:T(8,128)S(1)}, u32[]{:S(2)}, u32[]{:S(2)}) collective-permute-start(f32[192,128]{1,0:T(8,128)S(1)} %get-tuple-element.178), channel_id=1, source_target_pairs={{0,8},{1,9},{2,10},{3,11},{4,12},{5,13},{6,14},{7,15},{8,0},{9,1},... | collective-permute-start | bytes 294920 | tf_op jit(solution)/shard_map/ppermute | solution.py:164
  208.4 3.0 %collective-permute-start.38 = (f32[96,640]{1,0:T(8,128)S(1)}, f32[96,640]{1,0:T(8,128)S(1)}, u32[]{:S(2)}, u32[]{:S(2)}) collective-permute-start(f32[96,640]{1,0:T(8,128)S(1)} %slice.157), channel_id=1, source_target_pairs={{0,2},{1,3},{2,0},{3,1},{4,6},{5,7},{6,4},{7,5},{8,10},{9,11},{10,... | collective-permute-start | bytes 737288 | tf_op jit(solution)/shard_map/ppermute | solution.py:164
  211.4 2.6 %collective-permute-start.37 = (f32[192,256]{1,0:T(8,128)S(1)}, f32[192,256]{1,0:T(8,128)S(1)}, u32[]{:S(2)}, u32[]{:S(2)}) collective-permute-start(f32[192,256]{1,0:T(8,128)S(1)} %slice.147), channel_id=1, source_target_pairs={{0,8},{1,9},{2,10},{3,11},{4,12},{5,13},{6,14},{7,15},{8,0},{9,1},... | collective-permute-start | bytes 589832 | tf_op jit(solution)/shard_map/ppermute | solution.py:164
  214.0 3.8 %collective-permute-done.37 = f32[192,256]{1,0:T(8,128)S(1)} collective-permute-done((f32[192,256]{1,0:T(8,128)S(1)}, f32[192,256]{1,0:T(8,128)S(1)}, u32[]{:S(2)}, u32[]{:S(2)}) %collective-permute-start.37) | collective-permute-done | bytes 196640 | tf_op jit(solution)/shard_map/ppermute | solution.py:164
  217.9 1.6 collective-permute-start.39
  (145 shorter events, 20.6 us)
Async XLA Ops:
  2.3 6.4 %copy-start.9 = (s32[16]{0:T(128)S(1)}, s32[16]{0:T(128)}, u32[]{:S(2)}) copy-start(s32[16]{0:T(128)} %constant.121.clone) | copy-start | bytes 196
  2.3 6.5 %copy-start.5 = (s32[32]{0:T(128)S(1)}, s32[32]{0:T(128)}, u32[]{:S(2)}) copy-start(s32[32]{0:T(128)} %param.13) | copy-start | bytes 388
  2.3 6.5 %copy-start.8 = (s32[32]{0:T(128)S(1)}, s32[32]{0:T(128)}, u32[]{:S(2)}) copy-start(s32[32]{0:T(128)} %param.12) | copy-start | bytes 388
  2.3 26.2 %collective-permute-start.1 = (f32[2112,128]{1,0:T(8,128)}, f32[2112,128]{1,0:T(8,128)}, u32[]{:S(2)}, u32[]{:S(2)}) collective-permute-start(f32[2112,128]{1,0:T(8,128)} %slice.153.t_ref), channel_id=1, source_target_pairs={{0,48},{16,0},{32,16},{48,32},{64,112},{80,64},{96,80},{112,96},{1... | collective-permute-start | bytes 3244040 | tf_op jit(solution)/shard_map/ppermute | solution.py:198
  5.6 24.7 %collective-permute-start.2 = (f32[2112,128]{1,0:T(8,128)}, f32[2112,128]{1,0:T(8,128)}, u32[]{:S(2)}, u32[]{:S(2)}) collective-permute-start(f32[2112,128]{1,0:T(8,128)} %slice.153.t_ref), channel_id=1, source_target_pairs={{0,64},{16,80},{32,96},{48,112},{64,0},{80,16},{96,32},{112,48},{1... | collective-permute-start | bytes 3244040 | tf_op jit(solution)/shard_map/ppermute | solution.py:198
  8.6 10.3 %copy-start.2 = (f32[2144,128]{1,0:T(8,128)}, f32[2144,128]{1,0:T(8,128)S(1)}, u32[]{:S(2)}) copy-start(f32[2144,128]{1,0:T(8,128)S(1)} %get-tuple-element.96.t_ref) | copy-start | bytes 3293188
  8.6 25.9 %collective-permute-start = (f32[2144,128]{1,0:T(8,128)S(1)}, f32[2144,128]{1,0:T(8,128)}, u32[]{:S(2)}, u32[]{:S(2)}) collective-permute-start(f32[2144,128]{1,0:T(8,128)S(1)} %get-tuple-element.107.t_ref), channel_id=1, source_target_pairs={{0,16},{16,32},{32,48},{48,0},{64,80},{80,96},{96,112},{112,64},{1... | collective-permute-start | bytes 3293192 | tf_op jit(solution)/shard_map/ppermute | solution.py:198
  9.0 4.7 %copy-start = (f32[8,800,512]{2,1,0:T(8,128)S(1)}, f32[8,800,512]{2,1,0:T(8,128)}, u32[]{:S(2)}) copy-start(f32[8,800,512]{2,1,0:T(8,128)} %param.9) | copy-start | bytes 39321604
  21.1 13.5 %copy-start.3 = (f32[2144,128]{1,0:T(8,128)S(1)}, f32[2144,128]{1,0:T(8,128)}, u32[]{:S(2)}) copy-start(f32[2144,128]{1,0:T(8,128)} %copy-done.2) | copy-start | bytes 3293188
  34.5 24.5 %collective-permute-start.5 = (f32[2144,128]{1,0:T(8,128)}, f32[2144,128]{1,0:T(8,128)S(1)}, u32[]{:S(2)}, u32[]{:S(2)}) collective-permute-start(f32[2144,128]{1,0:T(8,128)} %collective-permute-done.t_ref), channel_id=1, source_target_pairs={{0,64},{16,80},{32,96},{48,112},{64,0},{80,16},{96,32},{112,48},{1... | collective-permute-start | bytes 3293192 | tf_op jit(solution)/shard_map/ppermute | solution.py:198
  34.6 24.3 %collective-permute-start.4 = (f32[2144,128]{1,0:T(8,128)S(1)}, f32[2144,128]{1,0:T(8,128)S(1)}, u32[]{:S(2)}, u32[]{:S(2)}) collective-permute-start(f32[2144,128]{1,0:T(8,128)S(1)} %copy-done.3), channel_id=1, source_target_pairs={{0,48},{16,0},{32,16},{48,32},{64,112},{80,64},{96,80},{112,96},{1... | collective-permute-start | bytes 3293192 | tf_op jit(solution)/shard_map/ppermute | solution.py:198
  34.6 24.3 %collective-permute-start.3 = (f32[2112,128]{1,0:T(8,128)}, f32[2112,128]{1,0:T(8,128)S(1)}, u32[]{:S(2)}, u32[]{:S(2)}) collective-permute-start(f32[2112,128]{1,0:T(8,128)} %slice.153.t_ref), channel_id=1, source_target_pairs={{0,16},{16,32},{32,48},{48,0},{64,80},{80,96},{96,112},{112,64},{1... | collective-permute-start | bytes 3244040 | tf_op jit(solution)/shard_map/ppermute | solution.py:198
  36.1 17.6 %collective-permute-start.6 = (f32[768,128]{1,0:T(8,128)S(1)}, f32[768,128]{1,0:T(8,128)S(1)}, u32[]{:S(2)}, u32[]{:S(2)}) collective-permute-start(f32[768,128]{1,0:T(8,128)S(1)} %slice.119), channel_id=1, source_target_pairs={{0,1},{1,0},{2,3},{3,2},{4,5},{5,4},{6,7},{7,6},{8,9},{9,8},{10,11... | collective-permute-start | bytes 1179656 | tf_op jit(solution)/shard_map/ppermute | solution.py:164
  39.2 4.7 %copy-start.1 = (f32[8,800,512]{2,1,0:T(8,128)S(1)}, f32[8,800,512]{2,1,0:T(8,128)}, u32[]{:S(2)}) copy-start(f32[8,800,512]{2,1,0:T(8,128)} %param.9) | copy-start | bytes 39321604
  59.0 23.6 %collective-permute-start.7 = (f32[2144,128]{1,0:T(8,128)S(1)}, f32[2144,128]{1,0:T(8,128)S(1)}, u32[]{:S(2)}, u32[]{:S(2)}) collective-permute-start(f32[2144,128]{1,0:T(8,128)S(1)} %copy-done.3), channel_id=1, source_target_pairs={{0,16},{16,32},{32,48},{48,0},{64,80},{80,96},{96,112},{112,64},{1... | collective-permute-start | bytes 3293192 | tf_op jit(solution)/shard_map/ppermute | solution.py:198
  59.0 23.5 %collective-permute-start.8 = (f32[2144,128]{1,0:T(8,128)S(1)}, f32[2144,128]{1,0:T(8,128)S(1)}, u32[]{:S(2)}, u32[]{:S(2)}) collective-permute-start(f32[2144,128]{1,0:T(8,128)S(1)} %collective-permute-done.5.t_ref), channel_id=1, source_target_pairs={{0,48},{16,0},{32,16},{48,32},{64,112},{80,64},{96,80},{112,96},{1... | collective-permute-start | bytes 3293192 | tf_op jit(solution)/shard_map/ppermute | solution.py:198
  61.7 21.8 %collective-permute-start.9 = (f32[2144,128]{1,0:T(8,128)S(1)}, f32[2144,128]{1,0:T(8,128)S(1)}, u32[]{:S(2)}, u32[]{:S(2)}) collective-permute-start(f32[2144,128]{1,0:T(8,128)S(1)} %copy-done.3), channel_id=1, source_target_pairs={{0,64},{16,80},{32,96},{48,112},{64,0},{80,16},{96,32},{112,48},{1... | collective-permute-start | bytes 3293192 | tf_op jit(solution)/shard_map/ppermute | solution.py:198
  63.0 7.3 %collective-permute-start.10 = (f32[384,128]{1,0:T(8,128)S(1)}, f32[384,128]{1,0:T(8,128)S(1)}, u32[]{:S(2)}, u32[]{:S(2)}) collective-permute-start(f32[384,128]{1,0:T(8,128)S(1)} %slice.121), channel_id=1, source_target_pairs={{0,4},{1,5},{2,6},{3,7},{4,0},{5,1},{6,2},{7,3},{8,12},{9,13},{10,... | collective-permute-start | bytes 589832 | tf_op jit(solution)/shard_map/ppermute | solution.py:164
  66.3 21.1 %slice-start = ((s8[13107200]{0:T(1024)(128)(4,1)}), s8[4194304]{0:T(1024)(128)(4,1)S(1)}, s32[]{:S(2)}) async-start(s8[13107200]{0:T(1024)(128)(4,1)} %bitcast.23), calls=%async_computation | async-start | bytes 8388608
  66.3 21.1 %slice-start.1 = ((s8[13107200]{0:T(1024)(128)(4,1)}), s8[4194304]{0:T(1024)(128)(4,1)S(1)}, s32[]{:S(2)}) async-start(s8[13107200]{0:T(1024)(128)(4,1)} %bitcast.23), calls=%async_computation.1 | async-start | bytes 8388608
  67.9 19.5 %slice-start.2 = ((s8[13107200]{0:T(1024)(128)(4,1)}), s8[4194304]{0:T(1024)(128)(4,1)S(1)}, s32[]{:S(2)}) async-start(s8[13107200]{0:T(1024)(128)(4,1)} %bitcast.23), calls=%async_computation.2 | async-start | bytes 8388608
  68.0 19.5 %slice-start.3 = ((s8[13107200]{0:T(1024)(128)(4,1)}), s8[524288]{0:T(1024)(128)(4,1)S(1)}, s32[]{:S(2)}) async-start(s8[13107200]{0:T(1024)(128)(4,1)} %bitcast.23), calls=%async_computation.3 | async-start | bytes 1048576
  83.5 22.6 %collective-permute-start.11 = (f32[2144,128]{1,0:T(8,128)S(1)}, f32[2144,128]{1,0:T(8,128)S(1)}, u32[]{:S(2)}, u32[]{:S(2)}) collective-permute-start(f32[2144,128]{1,0:T(8,128)S(1)} %collective-permute-done.9.t_ref), channel_id=1, source_target_pairs={{0,16},{16,32},{32,48},{48,0},{64,80},{80,96},{96,112},{112,64},{1... | collective-permute-start | bytes 3293192 | tf_op jit(solution)/shard_map/ppermute | solution.py:198
  83.5 22.6 %collective-permute-start.12 = (f32[2144,128]{1,0:T(8,128)S(1)}, f32[2144,128]{1,0:T(8,128)S(1)}, u32[]{:S(2)}, u32[]{:S(2)}) collective-permute-start(f32[2144,128]{1,0:T(8,128)S(1)} %get-tuple-element.107.t_ref), channel_id=1, source_target_pairs={{0,48},{16,0},{32,16},{48,32},{64,112},{80,64},{96,80},{112,96},{1... | collective-permute-start | bytes 3293192 | tf_op jit(solution)/shard_map/ppermute | solution.py:198
  86.1 20.0 %collective-permute-start.13 = (f32[2112,128]{1,0:T(8,128)S(1)}, f32[2112,128]{1,0:T(8,128)S(1)}, u32[]{:S(2)}, u32[]{:S(2)}) collective-permute-start(f32[2112,128]{1,0:T(8,128)S(1)} %collective-permute-done.3.t_ref), channel_id=1, source_target_pairs={{0,64},{16,80},{32,96},{48,112},{64,0},{80,16},{96,32},{112,48},{1... | collective-permute-start | bytes 3244040 | tf_op jit(solution)/shard_map/ppermute | solution.py:198
  92.3 5.9 %collective-permute-start.14 = (f32[192,128]{1,0:T(8,128)S(1)}, f32[192,128]{1,0:T(8,128)S(1)}, u32[]{:S(2)}, u32[]{:S(2)}) collective-permute-start(f32[192,128]{1,0:T(8,128)S(1)} %slice.123), channel_id=1, source_target_pairs={{0,8},{1,9},{2,10},{3,11},{4,12},{5,13},{6,14},{7,15},{8,0},{9,1},... | collective-permute-start | bytes 294920 | tf_op jit(solution)/shard_map/ppermute | solution.py:164
  106.1 22.1 %collective-permute-start.15 = (f32[2144,128]{1,0:T(8,128)}, f32[2144,128]{1,0:T(8,128)S(1)}, u32[]{:S(2)}, u32[]{:S(2)}) collective-permute-start(f32[2144,128]{1,0:T(8,128)} %collective-permute-done.t_ref), channel_id=1, source_target_pairs={{0,16},{16,32},{32,48},{48,0},{64,80},{80,96},{96,112},{112,64},{1... | collective-permute-start | bytes 3293192 | tf_op jit(solution)/shard_map/ppermute | solution.py:198
  106.1 22.7 %collective-permute-start.17 = (f32[2144,128]{1,0:T(8,128)S(1)}, f32[2144,128]{1,0:T(8,128)S(1)}, u32[]{:S(2)}, u32[]{:S(2)}) collective-permute-start(f32[2144,128]{1,0:T(8,128)S(1)} %collective-permute-done.12.t_ref), channel_id=1, source_target_pairs={{0,64},{16,80},{32,96},{48,112},{64,0},{80,16},{96,32},{112,48},{1... | collective-permute-start | bytes 3293192 | tf_op jit(solution)/shard_map/ppermute | solution.py:198
  107.5 20.7 %collective-permute-start.16 = (f32[2112,128]{1,0:T(8,128)}, f32[2112,128]{1,0:T(8,128)S(1)}, u32[]{:S(2)}, u32[]{:S(2)}) collective-permute-start(f32[2112,128]{1,0:T(8,128)} %collective-permute-done.1.t_ref), channel_id=1, source_target_pairs={{0,48},{16,0},{32,16},{48,32},{64,112},{80,64},{96,80},{112,96},{1... | collective-permute-start | bytes 3244040 | tf_op jit(solution)/shard_map/ppermute | solution.py:198
  110.1 18.0 %collective-permute-start.18 = (f32[768,256]{1,0:T(8,128)S(1)}, f32[768,256]{1,0:T(8,128)S(1)}, u32[]{:S(2)}, u32[]{:S(2)}) collective-permute-start(f32[768,256]{1,0:T(8,128)S(1)} %slice.125), channel_id=1, source_target_pairs={{0,1},{1,0},{2,3},{3,2},{4,5},{5,4},{6,7},{7,6},{8,9},{9,8},{10,11... | collective-permute-start | bytes 2359304 | tf_op jit(solution)/shard_map/ppermute | solution.py:164
  128.8 27.1 %collective-permute-start.19 = (f32[2144,128]{1,0:T(8,128)S(1)}, f32[2144,128]{1,0:T(8,128)S(1)}, u32[]{:S(2)}, u32[]{:S(2)}) collective-permute-start(f32[2144,128]{1,0:T(8,128)S(1)} %collective-permute-done.7.t_ref), channel_id=1, source_target_pairs={{0,16},{16,32},{32,48},{48,0},{64,80},{80,96},{96,112},{112,64},{1... | collective-permute-start | bytes 3293192 | tf_op jit(solution)/shard_map/ppermute | solution.py:198
  129.2 26.7 %collective-permute-start.21 = (f32[2144,128]{1,0:T(8,128)S(1)}, f32[2144,128]{1,0:T(8,128)S(1)}, u32[]{:S(2)}, u32[]{:S(2)}) collective-permute-start(f32[2144,128]{1,0:T(8,128)S(1)} %collective-permute-done.4.t_ref), channel_id=1, source_target_pairs={{0,64},{16,80},{32,96},{48,112},{64,0},{80,16},{96,32},{112,48},{1... | collective-permute-start | bytes 3293192 | tf_op jit(solution)/shard_map/ppermute | solution.py:198
  130.4 25.5 %collective-permute-start.20 = (f32[2112,128]{1,0:T(8,128)}, f32[2112,128]{1,0:T(8,128)S(1)}, u32[]{:S(2)}, u32[]{:S(2)}) collective-permute-start(f32[2112,128]{1,0:T(8,128)} %collective-permute-done.2.t_ref), channel_id=1, source_target_pairs={{0,48},{16,0},{32,16},{48,32},{64,112},{80,64},{96,80},{112,96},{1... | collective-permute-start | bytes 3244040 | tf_op jit(solution)/shard_map/ppermute | solution.py:198
  132.8 22.9 %collective-permute-start.23 = (f32[768,256]{1,0:T(8,128)S(1)}, f32[768,256]{1,0:T(8,128)S(1)}, u32[]{:S(2)}, u32[]{:S(2)}) collective-permute-start(f32[768,256]{1,0:T(8,128)S(1)} %slice.129), channel_id=1, source_target_pairs={{0,1},{1,0},{2,3},{3,2},{4,5},{5,4},{6,7},{7,6},{8,9},{9,8},{10,11... | collective-permute-start | bytes 2359304 | tf_op jit(solution)/shard_map/ppermute | solution.py:164
  144.6 11.1 %collective-permute-start.22 = (f32[384,256]{1,0:T(8,128)S(1)}, f32[384,256]{1,0:T(8,128)S(1)}, u32[]{:S(2)}, u32[]{:S(2)}) collective-permute-start(f32[384,256]{1,0:T(8,128)S(1)} %slice.127), channel_id=1, source_target_pairs={{0,4},{1,5},{2,6},{3,7},{4,0},{5,1},{6,2},{7,3},{8,12},{9,13},{10,... | collective-permute-start | bytes 1179656 | tf_op jit(solution)/shard_map/ppermute | solution.py:164
  155.9 21.7 %collective-permute-start.25 = (f32[2144,128]{1,0:T(8,128)S(1)}, f32[2144,128]{1,0:T(8,128)S(1)}, u32[]{:S(2)}, u32[]{:S(2)}) collective-permute-start(f32[2144,128]{1,0:T(8,128)S(1)} %collective-permute-done.21.t_ref), channel_id=1, source_target_pairs={{0,48},{16,0},{32,16},{48,32},{64,112},{80,64},{96,80},{112,96},{1... | collective-permute-start | bytes 3293192 | tf_op jit(solution)/shard_map/ppermute | solution.py:198
  156.0 21.6 %collective-permute-start.26 = (f32[2144,128]{1,0:T(8,128)S(1)}, f32[2144,128]{1,0:T(8,128)S(1)}, u32[]{:S(2)}, u32[]{:S(2)}) collective-permute-start(f32[2144,128]{1,0:T(8,128)S(1)} %collective-permute-done.15.t_ref), channel_id=1, source_target_pairs={{0,64},{16,80},{32,96},{48,112},{64,0},{80,16},{96,32},{112,48},{1... | collective-permute-start | bytes 3293192 | tf_op jit(solution)/shard_map/ppermute | solution.py:198
  156.1 19.1 %collective-permute-start.24 = (f32[2112,128]{1,0:T(8,128)S(1)}, f32[2112,128]{1,0:T(8,128)S(1)}, u32[]{:S(2)}, u32[]{:S(2)}) collective-permute-start(f32[2112,128]{1,0:T(8,128)S(1)} %collective-permute-done.13.t_ref), channel_id=1, source_target_pairs={{0,16},{16,32},{32,48},{48,0},{64,80},{80,96},{96,112},{112,64},{1... | collective-permute-start | bytes 3244040 | tf_op jit(solution)/shard_map/ppermute | solution.py:198
  161.3 12.2 %collective-permute-start.28 = (f32[384,256]{1,0:T(8,128)S(1)}, f32[384,256]{1,0:T(8,128)S(1)}, u32[]{:S(2)}, u32[]{:S(2)}) collective-permute-start(f32[384,256]{1,0:T(8,128)S(1)} %slice.133), channel_id=1, source_target_pairs={{0,4},{1,5},{2,6},{3,7},{4,0},{5,1},{6,2},{7,3},{8,12},{9,13},{10,... | collective-permute-start | bytes 1179656 | tf_op jit(solution)/shard_map/ppermute | solution.py:164
  163.0 10.6 %collective-permute-start.27 = (f32[192,256]{1,0:T(8,128)S(1)}, f32[192,256]{1,0:T(8,128)S(1)}, u32[]{:S(2)}, u32[]{:S(2)}) collective-permute-start(f32[192,256]{1,0:T(8,128)S(1)} %slice.131), channel_id=1, source_target_pairs={{0,8},{1,9},{2,10},{3,11},{4,12},{5,13},{6,14},{7,15},{8,0},{9,1},... | collective-permute-start | bytes 589832 | tf_op jit(solution)/shard_map/ppermute | solution.py:164
  177.7 13.6 %collective-permute-start.29 = (f32[768,256]{1,0:T(8,128)S(1)}, f32[768,256]{1,0:T(8,128)S(1)}, u32[]{:S(2)}, u32[]{:S(2)}) collective-permute-start(f32[768,256]{1,0:T(8,128)S(1)} %slice.135), channel_id=1, source_target_pairs={{0,1},{1,0},{2,3},{3,2},{4,5},{5,4},{6,7},{7,6},{8,9},{9,8},{10,11... | collective-permute-start | bytes 2359304 | tf_op jit(solution)/shard_map/ppermute | solution.py:164
  191.4 8.6 %collective-permute-start.31 = (f32[192,256]{1,0:T(8,128)S(1)}, f32[192,256]{1,0:T(8,128)S(1)}, u32[]{:S(2)}, u32[]{:S(2)}) collective-permute-start(f32[192,256]{1,0:T(8,128)S(1)} %get-tuple-element.175), channel_id=1, source_target_pairs={{0,8},{1,9},{2,10},{3,11},{4,12},{5,13},{6,14},{7,15},{8,0},{9,1},... | collective-permute-start | bytes 589832 | tf_op jit(solution)/shard_map/ppermute | solution.py:164
  194.8 10.0 %collective-permute-start.32 = (f32[192,256]{1,0:T(8,128)S(1)}, f32[192,256]{1,0:T(8,128)S(1)}, u32[]{:S(2)}, u32[]{:S(2)}) collective-permute-start(f32[192,256]{1,0:T(8,128)S(1)} %get-tuple-element.177), channel_id=1, source_target_pairs={{0,4},{1,5},{2,6},{3,7},{4,0},{5,1},{6,2},{7,3},{8,12},{9,13},{10,... | collective-permute-start | bytes 589832 | tf_op jit(solution)/shard_map/ppermute | solution.py:164
  195.5 9.3 %collective-permute-start.33 = (f32[192,256]{1,0:T(8,128)S(1)}, f32[192,256]{1,0:T(8,128)S(1)}, u32[]{:S(2)}, u32[]{:S(2)}) collective-permute-start(f32[192,256]{1,0:T(8,128)S(1)} %get-tuple-element.176), channel_id=1, source_target_pairs={{0,12},{1,13},{2,14},{3,15},{4,8},{5,9},{6,10},{7,11},{8,4},{9,5},... | collective-permute-start | bytes 589832 | tf_op jit(solution)/shard_map/ppermute | solution.py:164
  195.5 9.3 %collective-permute-start.30 = (f32[768,128]{1,0:T(8,128)S(1)}, f32[768,128]{1,0:T(8,128)S(1)}, u32[]{:S(2)}, u32[]{:S(2)}) collective-permute-start(f32[768,128]{1,0:T(8,128)S(1)} %slice.137), channel_id=1, source_target_pairs={{0,1},{1,0},{2,3},{3,2},{4,5},{5,4},{6,7},{7,6},{8,9},{9,8},{10,11... | collective-permute-start | bytes 1179656 | tf_op jit(solution)/shard_map/ppermute | solution.py:164
  205.0 9.0 %collective-permute-start.34 = (f32[192,128]{1,0:T(8,128)S(1)}, f32[192,128]{1,0:T(8,128)S(1)}, u32[]{:S(2)}, u32[]{:S(2)}) collective-permute-start(f32[192,128]{1,0:T(8,128)S(1)} %get-tuple-element.178), channel_id=1, source_target_pairs={{0,8},{1,9},{2,10},{3,11},{4,12},{5,13},{6,14},{7,15},{8,0},{9,1},... | collective-permute-start | bytes 294920 | tf_op jit(solution)/shard_map/ppermute | solution.py:164
  207.6 6.4 %collective-permute-start.35 = (f32[192,128]{1,0:T(8,128)S(1)}, f32[192,128]{1,0:T(8,128)S(1)}, u32[]{:S(2)}, u32[]{:S(2)}) collective-permute-start(f32[192,128]{1,0:T(8,128)S(1)} %get-tuple-element.180), channel_id=1, source_target_pairs={{0,4},{1,5},{2,6},{3,7},{4,0},{5,1},{6,2},{7,3},{8,12},{9,13},{10,... | collective-permute-start | bytes 294920 | tf_op jit(solution)/shard_map/ppermute | solution.py:164
  208.3 5.6 %collective-permute-start.36 = (f32[192,128]{1,0:T(8,128)S(1)}, f32[192,128]{1,0:T(8,128)S(1)}, u32[]{:S(2)}, u32[]{:S(2)}) collective-permute-start(f32[192,128]{1,0:T(8,128)S(1)} %get-tuple-element.179), channel_id=1, source_target_pairs={{0,12},{1,13},{2,14},{3,15},{4,8},{5,9},{6,10},{7,11},{8,4},{9,5},... | collective-permute-start | bytes 294920 | tf_op jit(solution)/shard_map/ppermute | solution.py:164
  208.4 9.5 %collective-permute-start.38 = (f32[96,640]{1,0:T(8,128)S(1)}, f32[96,640]{1,0:T(8,128)S(1)}, u32[]{:S(2)}, u32[]{:S(2)}) collective-permute-start(f32[96,640]{1,0:T(8,128)S(1)} %slice.157), channel_id=1, source_target_pairs={{0,2},{1,3},{2,0},{3,1},{4,6},{5,7},{6,4},{7,5},{8,10},{9,11},{10,... | collective-permute-start | bytes 737288 | tf_op jit(solution)/shard_map/ppermute | solution.py:164
  211.4 6.4 %collective-permute-start.37 = (f32[192,256]{1,0:T(8,128)S(1)}, f32[192,256]{1,0:T(8,128)S(1)}, u32[]{:S(2)}, u32[]{:S(2)}) collective-permute-start(f32[192,256]{1,0:T(8,128)S(1)} %slice.147), channel_id=1, source_target_pairs={{0,8},{1,9},{2,10},{3,11},{4,12},{5,13},{6,14},{7,15},{8,0},{9,1},... | collective-permute-start | bytes 589832 | tf_op jit(solution)/shard_map/ppermute | solution.py:164
  217.8 2.0 copy-start.4
  217.8 7.8 %copy-start.7 = (f32[512]{0:T(512)S(1)}, f32[512]{0:T(512)}, u32[]{:S(2)}) copy-start(f32[512]{0:T(512)} %param.10) | copy-start | bytes 6148
  217.9 7.8 %collective-permute-start.39 = (f32[96,384]{1,0:T(8,128)S(1)}, f32[96,384]{1,0:T(8,128)S(1)}, u32[]{:S(2)}, u32[]{:S(2)}) collective-permute-start(f32[96,384]{1,0:T(8,128)S(1)} %slice.159), channel_id=1, source_target_pairs={{0,2},{1,3},{2,0},{3,1},{4,6},{5,7},{6,4},{7,5},{8,10},{9,11},{10,... | collective-permute-start | bytes 442376 | tf_op jit(solution)/shard_map/ppermute | solution.py:164
  225.8 0.7 copy-start.6

commit v2 on v1

--- a/solution.py
+++ b/solution.py
@@ -8,13 +8,13 @@
 NX, NY = 4, 2
 STEPS = ((1, 0), (3, 0), (0, 1))
 ROUNDS = (
-    ((0, 1, (0, 0)), (1, 0, (0, 0)), (2, 0, (0, 0))),
-    ((0, 0, (0, 0)), (1, 2, (0, 0)), (2, 1, (1, 0))),
-    ((0, 2, (0, 0)), (1, 1, (1, 1)), (2, 2, (0, 0))),
-    ((0, 2, (0, 1)), (1, 1, (0, 0)), (2, 0, (1, 0))),
-    ((0, 1, (1, 0)), (1, 0, (3, 0)), (2, 1, (3, 0))),
-    ((0, 2, (1, 0)), (1, 0, (0, 1)), (2, 2, (3, 0))),
-    ((0, 0, (1, 1)), (1, 2, (3, 1)), (2, 1, (2, 0))),
+    ((0, 0, (0, 0)), (1, 0, (0, 0)), (2, 0, (0, 0))),
+    ((0, 2, (0, 0)), (1, 1, (0, 0)), (2, 2, (0, 0))),
+    ((0, 1, (0, 0)), (1, 2, (0, 0)), (2, 1, (3, 0))),
+    ((0, 1, (3, 1)), (1, 2, (0, 1)), (2, 0, (3, 0))),
+    ((0, 0, (0, 1)), (1, 2, (3, 0)), (2, 1, (1, 0))),
+    ((0, 0, (1, 0)), (1, 1, (3, 0)), (2, 2, (1, 0))),
+    ((0, 1, (1, 1)), (1, 0, (3, 1)), (2, 2, (2, 0))),
 )
 BATCHES = (
     {"blocks": 1, "pack": 0, "core": 1, "near": 2, "far": 3},

time: 230 us -> 226 us (0.983)
  waiting for transfers between devices: 61.8 us -> 56.7 us
    ppermute x21, waiting for transfers between devices: 42.1 us -> 37 us  [on_device(): lax.ppermute(held[p, offset], 'blk', link_pairs(STEPS[link]))]
    ppermute x19, starting transfers between devices: 58.7 us -> 56 us  [swap(): return lax.ppermute(part, 'vslab', [(i, i ^ bits) for i in range(owners)])]
    unnamed x30 -> x24, local copies, waits for them, and re-layouts: 10.1 us -> 11.4 us
  transfers between devices with their start and end apart: 40 -> 40, of which waited for: 15 -> 17; matrix products, arithmetic and copies ran while one was open for 2% -> 2% of each run, Pallas kernels for 26% -> 26%
where the time goes in v2:
time: 226 us; the launch traced here: 224 us
  starting transfers between devices  81.8 us (36%)
  Pallas kernels  59.2 us (26%)
  waiting for transfers between devices  56.7 us (25%)
  local copies, waits for them, and re-layouts  16.6 us (7%)
  between operations  5.95 us (3%)
  other arithmetic  3.34 us (1%)
    ppermute x19, starting transfers between devices, swap(): return lax.ppermute(part, 'vslab', [(i, i ^ bits) for i in range(owners)])  56 us
    pallas_call x24, Pallas kernels, product(): pl.pallas_call(product_kernel, grid=(steps,), in_specs=[pl.BlockSpec((til...  49.1 us
    ppermute x21, waiting for transfers between devices, on_device(): lax.ppermute(held[p, offset], 'blk', link_pairs(STEPS[link]))  37 us
    ppermute x21, starting transfers between devices, on_device(): lax.ppermute(held[p, offset], 'blk', link_pairs(STEPS[link]))  25.9 us
    ppermute x19, waiting for transfers between devices, swap(): return lax.ppermute(part, 'vslab', [(i, i ^ bits) for i in range(owners)])  19.6 us
    unnamed x24, local copies, waits for them, and re-layouts  11.4 us
    pallas_call x5, Pallas kernels, pack(): pl.pallas_call(pack_kernel, grid=(4,), in_specs=[pl.BlockSpec((tile, hot....  10.1 us
  transfers between devices with their start and end apart: 40, of which 17 were waited for; matrix products, arithmetic and copies ran while one was open for 2% of the time, Pallas kernels for 26%

profile of v2, /device:TPU:1, one launch (start us, length us, event | category | flops | bytes accessed | tf_op | source)
XLA Modules:
  0.0 223.6 jit_solution(15462164457266765387)
XLA Ops:
  0.0 2.3 %slice.153.t_ref = f32[2112,128]{1,0:T(8,128)} slice(f32[6400,128]{1,0:T(8,128)} %bitcast.38), slice={[0:2112], [0:128]} | slice | bytes 2162688 | tf_op jit(solution)/shard_map/slice | solution.py:141
  2.3 2.0 collective-permute-start
  5.6 1.5 collective-permute-start.2
  7.1 1.7 fusion.19
  8.8 5.1 %copy-done = f32[8,800,512]{2,1,0:T(8,128)S(1)} copy-done((f32[8,800,512]{2,1,0:T(8,128)S(1)}, f32[8,800,512]{2,1,0:T(8,128)}, u32[]{:S(2)}) %copy-start) | copy-done | bytes 13107224
  13.9 3.5 %product.24 = f32[128,512]{1,0:T(8,128)S(1)} custom-call(f32[2112,128]{1,0:T(8,128)} %slice.153.t_ref, f32[6400,512]{1,0:T(8,128)S(1)} %bitcast.14), custom_call_target="tpu_custom_call" | custom-call | flops 1 | bytes 1 | tf_op jit(solution)/shard_map/product/pallas_call | solution.py:89
  17.5 1.6 product.25
  19.2 1.6 product.26
  21.7 1.9 pack.5
  23.6 5.4 %collective-permute-done.t_ref = f32[2112,128]{1,0:T(8,128)} collective-permute-done((f32[2112,128]{1,0:T(8,128)}, f32[2112,128]{1,0:T(8,128)}, u32[]{:S(2)}, u32[]{:S(2)}) %collective-permute-start) | collective-permute-done | bytes 1081376 | tf_op jit(solution)/shard_map/ppermute | solution.py:198
  31.6 2.6 %collective-permute-start.4 = (f32[2144,128]{1,0:T(8,128)S(1)}, f32[2144,128]{1,0:T(8,128)S(1)}, u32[]{:S(2)}, u32[]{:S(2)}) collective-permute-start(f32[2144,128]{1,0:T(8,128)S(1)} %copy-done.4), channel_id=1, source_target_pairs={{0,48},{16,0},{32,16},{48,32},{64,112},{80,64},{96,80},{112,96},{1... | collective-permute-start | bytes 3293192 | tf_op jit(solution)/shard_map/ppermute | solution.py:198
  34.2 3.1 %collective-permute-start.6 = (f32[768,128]{1,0:T(8,128)S(1)}, f32[768,128]{1,0:T(8,128)S(1)}, u32[]{:S(2)}, u32[]{:S(2)}) collective-permute-start(f32[768,128]{1,0:T(8,128)S(1)} %slice.119), channel_id=1, source_target_pairs={{0,1},{1,0},{2,3},{3,2},{4,5},{5,4},{6,7},{7,6},{8,9},{9,8},{10,11... | collective-permute-start | bytes 1179656 | tf_op jit(solution)/shard_map/ppermute | solution.py:164
  37.3 4.7 %copy-done.1 = f32[8,800,512]{2,1,0:T(8,128)S(1)} copy-done((f32[8,800,512]{2,1,0:T(8,128)S(1)}, f32[8,800,512]{2,1,0:T(8,128)}, u32[]{:S(2)}) %copy-start.1) | copy-done | bytes 13107224
  42.0 4.1 %product.27 = f32[128,512]{1,0:T(8,128)S(1)} custom-call(f32[2112,128]{1,0:T(8,128)} %collective-permute-done.t_ref, f32[6400,512]{1,0:T(8,128)S(1)} %bitcast.17), custom_call_target="tpu_custom_call" | custom-call | flops 1 | bytes 1 | tf_op jit(solution)/shard_map/product/pallas_call | solution.py:89
  47.1 3.6 %product.28 = f32[128,512]{1,0:T(8,128)S(1)} custom-call(f32[2112,128]{1,0:T(8,128)} %collective-permute-done.1.t_ref, f32[6400,512]{1,0:T(8,128)S(1)} %bitcast.18), custom_call_target="tpu_custom_call" | custom-call | flops 1 | bytes 1 | tf_op jit(solution)/shard_map/product/pallas_call | solution.py:89
  50.6 3.6 %product.29 = f32[128,512]{1,0:T(8,128)S(1)} custom-call(f32[2112,128]{1,0:T(8,128)} %collective-permute-done.2.t_ref, f32[6400,512]{1,0:T(8,128)S(1)} %bitcast.19), custom_call_target="tpu_custom_call" | custom-call | flops 1 | bytes 1 | tf_op jit(solution)/shard_map/product/pallas_call | solution.py:89
  55.7 2.7 %collective-permute-start.8 = (f32[2144,128]{1,0:T(8,128)S(1)}, f32[2144,128]{1,0:T(8,128)S(1)}, u32[]{:S(2)}, u32[]{:S(2)}) collective-permute-start(f32[2144,128]{1,0:T(8,128)S(1)} %get-tuple-element.95.t_ref), channel_id=1, source_target_pairs={{0,48},{16,0},{32,16},{48,32},{64,112},{80,64},{96,80},{112,96},{1... | collective-permute-start | bytes 3293192 | tf_op jit(solution)/shard_map/ppermute | solution.py:198
  59.0 1.7 collective-permute-start.10
  60.7 1.6 product.31
  62.3 1.6 product.32
  63.9 1.6 product.30
  65.7 13.6 %collective-permute-done.7.t_ref = f32[2144,128]{1,0:T(8,128)S(1)} collective-permute-done((f32[2144,128]{1,0:T(8,128)S(1)}, f32[2144,128]{1,0:T(8,128)S(1)}, u32[]{:S(2)}, u32[]{:S(2)}) %collective-permute-start.7) | collective-permute-done | bytes 1097760 | tf_op jit(solution)/shard_map/ppermute | solution.py:198
  80.2 2.7 %collective-permute-start.12 = (f32[2144,128]{1,0:T(8,128)S(1)}, f32[2144,128]{1,0:T(8,128)S(1)}, u32[]{:S(2)}, u32[]{:S(2)}) collective-permute-start(f32[2144,128]{1,0:T(8,128)S(1)} %collective-permute-done.5.t_ref), channel_id=1, source_target_pairs={{0,48},{16,0},{32,16},{48,32},{64,112},{80,64},{96,80},{112,96},{1... | collective-permute-start | bytes 3293192 | tf_op jit(solution)/shard_map/ppermute | solution.py:198
  83.7 1.6 product.34
  85.3 1.6 product.35
  86.9 3.9 %collective-permute-start.14 = (f32[192,128]{1,0:T(8,128)S(1)}, f32[192,128]{1,0:T(8,128)S(1)}, u32[]{:S(2)}, u32[]{:S(2)}) collective-permute-start(f32[192,128]{1,0:T(8,128)S(1)} %slice.123), channel_id=1, source_target_pairs={{0,8},{1,9},{2,10},{3,11},{4,12},{5,13},{6,14},{7,15},{8,0},{9,1},... | collective-permute-start | bytes 294920 | tf_op jit(solution)/shard_map/ppermute | solution.py:164
  90.9 1.6 product.33
  92.5 2.1 pack.6
  94.7 8.4 %collective-permute-done.13.t_ref = f32[2112,128]{1,0:T(8,128)S(1)} collective-permute-done((f32[2112,128]{1,0:T(8,128)}, f32[2112,128]{1,0:T(8,128)S(1)}, u32[]{:S(2)}, u32[]{:S(2)}) %collective-permute-start.13) | collective-permute-done | bytes 1081376 | tf_op jit(solution)/shard_map/ppermute | solution.py:198
  103.0 1.6 collective-permute-start.16
  105.8 8.0 %collective-permute-start.18 = (f32[768,256]{1,0:T(8,128)S(1)}, f32[768,256]{1,0:T(8,128)S(1)}, u32[]{:S(2)}, u32[]{:S(2)}) collective-permute-start(f32[768,256]{1,0:T(8,128)S(1)} %slice.125), channel_id=1, source_target_pairs={{0,1},{1,0},{2,3},{3,2},{4,5},{5,4},{6,7},{7,6},{8,9},{9,8},{10,11... | collective-permute-start | bytes 2359304 | tf_op jit(solution)/shard_map/ppermute | solution.py:164
  113.9 1.6 product.36
  115.5 1.6 product.37
  117.1 2.2 product.38
  119.4 2.1 pack.7
  121.7 3.2 %collective-permute-done.15.t_ref = f32[2112,128]{1,0:T(8,128)S(1)} collective-permute-done((f32[2112,128]{1,0:T(8,128)}, f32[2112,128]{1,0:T(8,128)S(1)}, u32[]{:S(2)}, u32[]{:S(2)}) %collective-permute-start.15) | collective-permute-done | bytes 1081376 | tf_op jit(solution)/shard_map/ppermute | solution.py:198
  125.5 1.8 collective-permute-start.20
  128.5 9.7 %collective-permute-start.23 = (f32[768,256]{1,0:T(8,128)S(1)}, f32[768,256]{1,0:T(8,128)S(1)}, u32[]{:S(2)}, u32[]{:S(2)}) collective-permute-start(f32[768,256]{1,0:T(8,128)S(1)} %slice.129), channel_id=1, source_target_pairs={{0,1},{1,0},{2,3},{3,2},{4,5},{5,4},{6,7},{7,6},{8,9},{9,8},{10,11... | collective-permute-start | bytes 2359304 | tf_op jit(solution)/shard_map/ppermute | solution.py:164
  138.3 1.7 collective-permute-start.22
  140.0 2.2 product.39
  142.2 1.6 product.40
  143.8 1.6 product.41
  145.4 3.9 %collective-permute-done.22 = f32[384,256]{1,0:T(8,128)S(1)} collective-permute-done((f32[384,256]{1,0:T(8,128)S(1)}, f32[384,256]{1,0:T(8,128)S(1)}, u32[]{:S(2)}, u32[]{:S(2)}) %collective-permute-start.22) | collective-permute-done | bytes 393248 | tf_op jit(solution)/shard_map/ppermute | solution.py:164
  150.6 2.7 %collective-permute-start.25 = (f32[2112,128]{1,0:T(8,128)S(1)}, f32[2112,128]{1,0:T(8,128)S(1)}, u32[]{:S(2)}, u32[]{:S(2)}) collective-permute-start(f32[2112,128]{1,0:T(8,128)S(1)} %collective-permute-done.13.t_ref), channel_id=1, source_target_pairs={{0,48},{16,0},{32,16},{48,32},{64,112},{80,64},{96,80},{112,96},{1... | collective-permute-start | bytes 3244040 | tf_op jit(solution)/shard_map/ppermute | solution.py:198
  153.3 2.2 product.43
  155.5 1.6 product.44
  157.2 1.4 collective-permute-start.28
  158.6 3.6 %collective-permute-start.27 = (f32[192,256]{1,0:T(8,128)S(1)}, f32[192,256]{1,0:T(8,128)S(1)}, u32[]{:S(2)}, u32[]{:S(2)}) collective-permute-start(f32[192,256]{1,0:T(8,128)S(1)} %slice.131), channel_id=1, source_target_pairs={{0,8},{1,9},{2,10},{3,11},{4,12},{5,13},{6,14},{7,15},{8,0},{9,1},... | collective-permute-start | bytes 589832 | tf_op jit(solution)/shard_map/ppermute | solution.py:164
  162.3 1.6 product.42
  164.0 2.1 pack.8
  166.1 3.1 %collective-permute-done.27 = f32[192,256]{1,0:T(8,128)S(1)} collective-permute-done((f32[192,256]{1,0:T(8,128)S(1)}, f32[192,256]{1,0:T(8,128)S(1)}, u32[]{:S(2)}, u32[]{:S(2)}) %collective-permute-start.27) | collective-permute-done | bytes 196640 | tf_op jit(solution)/shard_map/ppermute | solution.py:164
  169.3 2.4 %collective-permute-done.24.t_ref = f32[2144,128]{1,0:T(8,128)S(1)} collective-permute-done((f32[2144,128]{1,0:T(8,128)S(1)}, f32[2144,128]{1,0:T(8,128)S(1)}, u32[]{:S(2)}, u32[]{:S(2)}) %collective-permute-start.24) | collective-permute-done | bytes 1097760 | tf_op jit(solution)/shard_map/ppermute | solution.py:198
  172.5 9.6 %collective-permute-start.29 = (f32[768,256]{1,0:T(8,128)S(1)}, f32[768,256]{1,0:T(8,128)S(1)}, u32[]{:S(2)}, u32[]{:S(2)}) collective-permute-start(f32[768,256]{1,0:T(8,128)S(1)} %slice.135), channel_id=1, source_target_pairs={{0,1},{1,0},{2,3},{3,2},{4,5},{5,4},{6,7},{7,6},{8,9},{9,8},{10,11... | collective-permute-start | bytes 2359304 | tf_op jit(solution)/shard_map/ppermute | solution.py:164
  182.0 1.6 product.45
  183.6 2.2 product.46
  185.8 1.6 product.47
  187.5 1.9 pack.9
  189.6 2.0 collective-permute-start.31
  193.9 3.8 %collective-permute-done.31 = f32[192,256]{1,0:T(8,128)S(1)} collective-permute-done((f32[192,256]{1,0:T(8,128)S(1)}, f32[192,256]{1,0:T(8,128)S(1)}, u32[]{:S(2)}, u32[]{:S(2)}) %collective-permute-start.31) | collective-permute-done | bytes 196640 | tf_op jit(solution)/shard_map/ppermute | solution.py:164
  197.7 3.9 %collective-permute-done.32 = f32[192,256]{1,0:T(8,128)S(1)} collective-permute-done((f32[192,256]{1,0:T(8,128)S(1)}, f32[192,256]{1,0:T(8,128)S(1)}, u32[]{:S(2)}, u32[]{:S(2)}) %collective-permute-start.32) | collective-permute-done | bytes 196640 | tf_op jit(solution)/shard_map/ppermute | solution.py:164
  202.4 2.0 collective-permute-start.34
  205.8 2.3 %collective-permute-start.38 = (f32[96,640]{1,0:T(8,128)S(1)}, f32[96,640]{1,0:T(8,128)S(1)}, u32[]{:S(2)}, u32[]{:S(2)}) collective-permute-start(f32[96,640]{1,0:T(8,128)S(1)} %slice.157), channel_id=1, source_target_pairs={{0,2},{1,3},{2,0},{3,1},{4,6},{5,7},{6,4},{7,5},{8,10},{9,11},{10,... | collective-permute-start | bytes 737288 | tf_op jit(solution)/shard_map/ppermute | solution.py:164
  208.2 2.1 collective-permute-start.37
  210.3 4.3 %collective-permute-done.37 = f32[192,256]{1,0:T(8,128)S(1)} collective-permute-done((f32[192,256]{1,0:T(8,128)S(1)}, f32[192,256]{1,0:T(8,128)S(1)}, u32[]{:S(2)}, u32[]{:S(2)}) %collective-permute-start.37) | collective-permute-done | bytes 196640 | tf_op jit(solution)/shard_map/ppermute | solution.py:164
  (139 shorter events, 23.9 us)
Async XLA Ops:
  2.3 26.8 %collective-permute-start = (f32[2112,128]{1,0:T(8,128)}, f32[2112,128]{1,0:T(8,128)}, u32[]{:S(2)}, u32[]{:S(2)}) collective-permute-start(f32[2112,128]{1,0:T(8,128)} %slice.153.t_ref), channel_id=1, source_target_pairs={{0,16},{16,32},{32,48},{48,0},{64,80},{80,96},{96,112},{112,64},{1... | collective-permute-start | bytes 3244040 | tf_op jit(solution)/shard_map/ppermute | solution.py:198
  4.3 24.7 %collective-permute-start.1 = (f32[2112,128]{1,0:T(8,128)}, f32[2112,128]{1,0:T(8,128)}, u32[]{:S(2)}, u32[]{:S(2)}) collective-permute-start(f32[2112,128]{1,0:T(8,128)} %slice.153.t_ref), channel_id=1, source_target_pairs={{0,48},{16,0},{32,16},{48,32},{64,112},{80,64},{96,80},{112,96},{1... | collective-permute-start | bytes 3244040 | tf_op jit(solution)/shard_map/ppermute | solution.py:198
  5.6 24.4 %collective-permute-start.2 = (f32[2112,128]{1,0:T(8,128)}, f32[2112,128]{1,0:T(8,128)}, u32[]{:S(2)}, u32[]{:S(2)}) collective-permute-start(f32[2112,128]{1,0:T(8,128)} %slice.153.t_ref), channel_id=1, source_target_pairs={{0,64},{16,80},{32,96},{48,112},{64,0},{80,16},{96,32},{112,48},{1... | collective-permute-start | bytes 3244040 | tf_op jit(solution)/shard_map/ppermute | solution.py:198
  8.8 8.7 %copy-start.3 = (f32[2144,128]{1,0:T(8,128)}, f32[2144,128]{1,0:T(8,128)S(1)}, u32[]{:S(2)}) copy-start(f32[2144,128]{1,0:T(8,128)S(1)} %get-tuple-element.94.t_ref) | copy-start | bytes 3293188
  8.8 5.1 %copy-start = (f32[8,800,512]{2,1,0:T(8,128)S(1)}, f32[8,800,512]{2,1,0:T(8,128)}, u32[]{:S(2)}) copy-start(f32[8,800,512]{2,1,0:T(8,128)} %param.9) | copy-start | bytes 39321604
  19.1 1.7 copy-start.10
  19.1 1.8 copy-start.6
  19.1 1.8 copy-start.9
  21.6 9.9 %copy-start.4 = (f32[2144,128]{1,0:T(8,128)S(1)}, f32[2144,128]{1,0:T(8,128)}, u32[]{:S(2)}) copy-start(f32[2144,128]{1,0:T(8,128)} %copy-done.3) | copy-start | bytes 3293188
  30.0 24.7 %collective-permute-start.3 = (f32[2144,128]{1,0:T(8,128)S(1)}, f32[2144,128]{1,0:T(8,128)S(1)}, u32[]{:S(2)}, u32[]{:S(2)}) collective-permute-start(f32[2144,128]{1,0:T(8,128)S(1)} %get-tuple-element.95.t_ref), channel_id=1, source_target_pairs={{0,16},{16,32},{32,48},{48,0},{64,80},{80,96},{96,112},{112,64},{1... | collective-permute-start | bytes 3293192 | tf_op jit(solution)/shard_map/ppermute | solution.py:198
  30.3 24.5 %collective-permute-start.5 = (f32[2144,128]{1,0:T(8,128)S(1)}, f32[2144,128]{1,0:T(8,128)S(1)}, u32[]{:S(2)}, u32[]{:S(2)}) collective-permute-start(f32[2144,128]{1,0:T(8,128)S(1)} %get-tuple-element.95.t_ref), channel_id=1, source_target_pairs={{0,64},{16,80},{32,96},{48,112},{64,0},{80,16},{96,32},{112,48},{1... | collective-permute-start | bytes 3293192 | tf_op jit(solution)/shard_map/ppermute | solution.py:198
  31.6 23.4 %collective-permute-start.4 = (f32[2144,128]{1,0:T(8,128)S(1)}, f32[2144,128]{1,0:T(8,128)S(1)}, u32[]{:S(2)}, u32[]{:S(2)}) collective-permute-start(f32[2144,128]{1,0:T(8,128)S(1)} %copy-done.4), channel_id=1, source_target_pairs={{0,48},{16,0},{32,16},{48,32},{64,112},{80,64},{96,80},{112,96},{1... | collective-permute-start | bytes 3293192 | tf_op jit(solution)/shard_map/ppermute | solution.py:198
  34.2 20.0 %collective-permute-start.6 = (f32[768,128]{1,0:T(8,128)S(1)}, f32[768,128]{1,0:T(8,128)S(1)}, u32[]{:S(2)}, u32[]{:S(2)}) collective-permute-start(f32[768,128]{1,0:T(8,128)S(1)} %slice.119), channel_id=1, source_target_pairs={{0,1},{1,0},{2,3},{3,2},{4,5},{5,4},{6,7},{7,6},{8,9},{9,8},{10,11... | collective-permute-start | bytes 1179656 | tf_op jit(solution)/shard_map/ppermute | solution.py:164
  37.3 4.7 %copy-start.1 = (f32[8,800,512]{2,1,0:T(8,128)S(1)}, f32[8,800,512]{2,1,0:T(8,128)}, u32[]{:S(2)}) copy-start(f32[8,800,512]{2,1,0:T(8,128)} %param.9) | copy-start | bytes 39321604
  42.0 5.0 %copy-start.2 = (f32[8,800,512]{2,1,0:T(8,128)S(1)}, f32[8,800,512]{2,1,0:T(8,128)}, u32[]{:S(2)}) copy-start(f32[8,800,512]{2,1,0:T(8,128)} %param.9) | copy-start | bytes 39321604
  55.0 24.3 %collective-permute-start.7 = (f32[2144,128]{1,0:T(8,128)S(1)}, f32[2144,128]{1,0:T(8,128)S(1)}, u32[]{:S(2)}, u32[]{:S(2)}) collective-permute-start(f32[2144,128]{1,0:T(8,128)S(1)} %copy-done.4), channel_id=1, source_target_pairs={{0,16},{16,32},{32,48},{48,0},{64,80},{80,96},{96,112},{112,64},{1... | collective-permute-start | bytes 3293192 | tf_op jit(solution)/shard_map/ppermute | solution.py:198
  55.7 23.6 %collective-permute-start.8 = (f32[2144,128]{1,0:T(8,128)S(1)}, f32[2144,128]{1,0:T(8,128)S(1)}, u32[]{:S(2)}, u32[]{:S(2)}) collective-permute-start(f32[2144,128]{1,0:T(8,128)S(1)} %get-tuple-element.95.t_ref), channel_id=1, source_target_pairs={{0,48},{16,0},{32,16},{48,32},{64,112},{80,64},{96,80},{112,96},{1... | collective-permute-start | bytes 3293192 | tf_op jit(solution)/shard_map/ppermute | solution.py:198
  58.4 21.8 %collective-permute-start.9 = (f32[2144,128]{1,0:T(8,128)S(1)}, f32[2144,128]{1,0:T(8,128)S(1)}, u32[]{:S(2)}, u32[]{:S(2)}) collective-permute-start(f32[2144,128]{1,0:T(8,128)S(1)} %collective-permute-done.4.t_ref), channel_id=1, source_target_pairs={{0,64},{16,80},{32,96},{48,112},{64,0},{80,16},{96,32},{112,48},{1... | collective-permute-start | bytes 3293192 | tf_op jit(solution)/shard_map/ppermute | solution.py:198
  59.0 6.7 %collective-permute-start.10 = (f32[384,128]{1,0:T(8,128)S(1)}, f32[384,128]{1,0:T(8,128)S(1)}, u32[]{:S(2)}, u32[]{:S(2)}) collective-permute-start(f32[384,128]{1,0:T(8,128)S(1)} %slice.121), channel_id=1, source_target_pairs={{0,4},{1,5},{2,6},{3,7},{4,0},{5,1},{6,2},{7,3},{8,12},{9,13},{10,... | collective-permute-start | bytes 589832 | tf_op jit(solution)/shard_map/ppermute | solution.py:164
  80.2 22.8 %collective-permute-start.11 = (f32[2144,128]{1,0:T(8,128)S(1)}, f32[2144,128]{1,0:T(8,128)S(1)}, u32[]{:S(2)}, u32[]{:S(2)}) collective-permute-start(f32[2144,128]{1,0:T(8,128)S(1)} %collective-permute-done.9.t_ref), channel_id=1, source_target_pairs={{0,16},{16,32},{32,48},{48,0},{64,80},{80,96},{96,112},{112,64},{1... | collective-permute-start | bytes 3293192 | tf_op jit(solution)/shard_map/ppermute | solution.py:198
  80.2 22.8 %collective-permute-start.12 = (f32[2144,128]{1,0:T(8,128)S(1)}, f32[2144,128]{1,0:T(8,128)S(1)}, u32[]{:S(2)}, u32[]{:S(2)}) collective-permute-start(f32[2144,128]{1,0:T(8,128)S(1)} %collective-permute-done.5.t_ref), channel_id=1, source_target_pairs={{0,48},{16,0},{32,16},{48,32},{64,112},{80,64},{96,80},{112,96},{1... | collective-permute-start | bytes 3293192 | tf_op jit(solution)/shard_map/ppermute | solution.py:198
  82.9 20.2 %collective-permute-start.13 = (f32[2112,128]{1,0:T(8,128)}, f32[2112,128]{1,0:T(8,128)S(1)}, u32[]{:S(2)}, u32[]{:S(2)}) collective-permute-start(f32[2112,128]{1,0:T(8,128)} %collective-permute-done.1.t_ref), channel_id=1, source_target_pairs={{0,64},{16,80},{32,96},{48,112},{64,0},{80,16},{96,32},{112,48},{1... | collective-permute-start | bytes 3244040 | tf_op jit(solution)/shard_map/ppermute | solution.py:198
  86.9 7.7 %collective-permute-start.14 = (f32[192,128]{1,0:T(8,128)S(1)}, f32[192,128]{1,0:T(8,128)S(1)}, u32[]{:S(2)}, u32[]{:S(2)}) collective-permute-start(f32[192,128]{1,0:T(8,128)S(1)} %slice.123), channel_id=1, source_target_pairs={{0,8},{1,9},{2,10},{3,11},{4,12},{5,13},{6,14},{7,15},{8,0},{9,1},... | collective-permute-start | bytes 294920 | tf_op jit(solution)/shard_map/ppermute | solution.py:164
  103.0 21.8 %collective-permute-start.16 = (f32[2144,128]{1,0:T(8,128)S(1)}, f32[2144,128]{1,0:T(8,128)S(1)}, u32[]{:S(2)}, u32[]{:S(2)}) collective-permute-start(f32[2144,128]{1,0:T(8,128)S(1)} %collective-permute-done.8.t_ref), channel_id=1, source_target_pairs={{0,48},{16,0},{32,16},{48,32},{64,112},{80,64},{96,80},{112,96},{1... | collective-permute-start | bytes 3293192 | tf_op jit(solution)/shard_map/ppermute | solution.py:198
  104.7 20.9 %collective-permute-start.17 = (f32[2144,128]{1,0:T(8,128)S(1)}, f32[2144,128]{1,0:T(8,128)S(1)}, u32[]{:S(2)}, u32[]{:S(2)}) collective-permute-start(f32[2144,128]{1,0:T(8,128)S(1)} %collective-permute-done.7.t_ref), channel_id=1, source_target_pairs={{0,64},{16,80},{32,96},{48,112},{64,0},{80,16},{96,32},{112,48},{1... | collective-permute-start | bytes 3293192 | tf_op jit(solution)/shard_map/ppermute | solution.py:198
  105.8 19.1 %collective-permute-start.15 = (f32[2112,128]{1,0:T(8,128)}, f32[2112,128]{1,0:T(8,128)S(1)}, u32[]{:S(2)}, u32[]{:S(2)}) collective-permute-start(f32[2112,128]{1,0:T(8,128)} %collective-permute-done.2.t_ref), channel_id=1, source_target_pairs={{0,16},{16,32},{32,48},{48,0},{64,80},{80,96},{96,112},{112,64},{1... | collective-permute-start | bytes 3244040 | tf_op jit(solution)/shard_map/ppermute | solution.py:198
  105.8 15.7 %collective-permute-start.18 = (f32[768,256]{1,0:T(8,128)S(1)}, f32[768,256]{1,0:T(8,128)S(1)}, u32[]{:S(2)}, u32[]{:S(2)}) collective-permute-start(f32[768,256]{1,0:T(8,128)S(1)} %slice.125), channel_id=1, source_target_pairs={{0,1},{1,0},{2,3},{3,2},{4,5},{5,4},{6,7},{7,6},{8,9},{9,8},{10,11... | collective-permute-start | bytes 2359304 | tf_op jit(solution)/shard_map/ppermute | solution.py:164
  125.5 24.0 %collective-permute-start.20 = (f32[2144,128]{1,0:T(8,128)S(1)}, f32[2144,128]{1,0:T(8,128)S(1)}, u32[]{:S(2)}, u32[]{:S(2)}) collective-permute-start(f32[2144,128]{1,0:T(8,128)S(1)} %collective-permute-done.4.t_ref), channel_id=1, source_target_pairs={{0,48},{16,0},{32,16},{48,32},{64,112},{80,64},{96,80},{112,96},{1... | collective-permute-start | bytes 3293192 | tf_op jit(solution)/shard_map/ppermute | solution.py:198
  127.3 22.2 %collective-permute-start.21 = (f32[2144,128]{1,0:T(8,128)S(1)}, f32[2144,128]{1,0:T(8,128)S(1)}, u32[]{:S(2)}, u32[]{:S(2)}) collective-permute-start(f32[2144,128]{1,0:T(8,128)S(1)} %collective-permute-done.3.t_ref), channel_id=1, source_target_pairs={{0,64},{16,80},{32,96},{48,112},{64,0},{80,16},{96,32},{112,48},{1... | collective-permute-start | bytes 3293192 | tf_op jit(solution)/shard_map/ppermute | solution.py:198
  128.4 21.1 %collective-permute-start.19 = (f32[2112,128]{1,0:T(8,128)}, f32[2112,128]{1,0:T(8,128)S(1)}, u32[]{:S(2)}, u32[]{:S(2)}) collective-permute-start(f32[2112,128]{1,0:T(8,128)} %collective-permute-done.t_ref), channel_id=1, source_target_pairs={{0,16},{16,32},{32,48},{48,0},{64,80},{80,96},{96,112},{112,64},{1... | collective-permute-start | bytes 3244040 | tf_op jit(solution)/shard_map/ppermute | solution.py:198
  128.5 20.9 %collective-permute-start.23 = (f32[768,256]{1,0:T(8,128)S(1)}, f32[768,256]{1,0:T(8,128)S(1)}, u32[]{:S(2)}, u32[]{:S(2)}) collective-permute-start(f32[768,256]{1,0:T(8,128)S(1)} %slice.129), channel_id=1, source_target_pairs={{0,1},{1,0},{2,3},{3,2},{4,5},{5,4},{6,7},{7,6},{8,9},{9,8},{10,11... | collective-permute-start | bytes 2359304 | tf_op jit(solution)/shard_map/ppermute | solution.py:164
  138.3 11.1 %collective-permute-start.22 = (f32[384,256]{1,0:T(8,128)S(1)}, f32[384,256]{1,0:T(8,128)S(1)}, u32[]{:S(2)}, u32[]{:S(2)}) collective-permute-start(f32[384,256]{1,0:T(8,128)S(1)} %slice.127), channel_id=1, source_target_pairs={{0,4},{1,5},{2,6},{3,7},{4,0},{5,1},{6,2},{7,3},{8,12},{9,13},{10,... | collective-permute-start | bytes 1179656 | tf_op jit(solution)/shard_map/ppermute | solution.py:164
  149.6 22.1 %collective-permute-start.24 = (f32[2144,128]{1,0:T(8,128)S(1)}, f32[2144,128]{1,0:T(8,128)S(1)}, u32[]{:S(2)}, u32[]{:S(2)}) collective-permute-start(f32[2144,128]{1,0:T(8,128)S(1)} %collective-permute-done.17.t_ref), channel_id=1, source_target_pairs={{0,16},{16,32},{32,48},{48,0},{64,80},{80,96},{96,112},{112,64},{1... | collective-permute-start | bytes 3293192 | tf_op jit(solution)/shard_map/ppermute | solution.py:198
  149.7 22.7 %collective-permute-start.26 = (f32[2144,128]{1,0:T(8,128)S(1)}, f32[2144,128]{1,0:T(8,128)S(1)}, u32[]{:S(2)}, u32[]{:S(2)}) collective-permute-start(f32[2144,128]{1,0:T(8,128)S(1)} %collective-permute-done.16.t_ref), channel_id=1, source_target_pairs={{0,64},{16,80},{32,96},{48,112},{64,0},{80,16},{96,32},{112,48},{1... | collective-permute-start | bytes 3293192 | tf_op jit(solution)/shard_map/ppermute | solution.py:198
  150.6 18.6 %collective-permute-start.25 = (f32[2112,128]{1,0:T(8,128)S(1)}, f32[2112,128]{1,0:T(8,128)S(1)}, u32[]{:S(2)}, u32[]{:S(2)}) collective-permute-start(f32[2112,128]{1,0:T(8,128)S(1)} %collective-permute-done.13.t_ref), channel_id=1, source_target_pairs={{0,48},{16,0},{32,16},{48,32},{64,112},{80,64},{96,80},{112,96},{1... | collective-permute-start | bytes 3244040 | tf_op jit(solution)/shard_map/ppermute | solution.py:198
  157.2 12.0 %collective-permute-start.28 = (f32[384,256]{1,0:T(8,128)S(1)}, f32[384,256]{1,0:T(8,128)S(1)}, u32[]{:S(2)}, u32[]{:S(2)}) collective-permute-start(f32[384,256]{1,0:T(8,128)S(1)} %slice.133), channel_id=1, source_target_pairs={{0,4},{1,5},{2,6},{3,7},{4,0},{5,1},{6,2},{7,3},{8,12},{9,13},{10,... | collective-permute-start | bytes 1179656 | tf_op jit(solution)/shard_map/ppermute | solution.py:164
  158.6 10.6 %collective-permute-start.27 = (f32[192,256]{1,0:T(8,128)S(1)}, f32[192,256]{1,0:T(8,128)S(1)}, u32[]{:S(2)}, u32[]{:S(2)}) collective-permute-start(f32[192,256]{1,0:T(8,128)S(1)} %slice.131), channel_id=1, source_target_pairs={{0,8},{1,9},{2,10},{3,11},{4,12},{5,13},{6,14},{7,15},{8,0},{9,1},... | collective-permute-start | bytes 589832 | tf_op jit(solution)/shard_map/ppermute | solution.py:164
  172.5 17.0 %collective-permute-start.29 = (f32[768,256]{1,0:T(8,128)S(1)}, f32[768,256]{1,0:T(8,128)S(1)}, u32[]{:S(2)}, u32[]{:S(2)}) collective-permute-start(f32[768,256]{1,0:T(8,128)S(1)} %slice.135), channel_id=1, source_target_pairs={{0,1},{1,0},{2,3},{3,2},{4,5},{5,4},{6,7},{7,6},{8,9},{9,8},{10,11... | collective-permute-start | bytes 2359304 | tf_op jit(solution)/shard_map/ppermute | solution.py:164
  189.6 8.1 %collective-permute-start.31 = (f32[192,256]{1,0:T(8,128)S(1)}, f32[192,256]{1,0:T(8,128)S(1)}, u32[]{:S(2)}, u32[]{:S(2)}) collective-permute-start(f32[192,256]{1,0:T(8,128)S(1)} %get-tuple-element.175), channel_id=1, source_target_pairs={{0,8},{1,9},{2,10},{3,11},{4,12},{5,13},{6,14},{7,15},{8,0},{9,1},... | collective-permute-start | bytes 589832 | tf_op jit(solution)/shard_map/ppermute | solution.py:164
  191.6 10.0 %collective-permute-start.32 = (f32[192,256]{1,0:T(8,128)S(1)}, f32[192,256]{1,0:T(8,128)S(1)}, u32[]{:S(2)}, u32[]{:S(2)}) collective-permute-start(f32[192,256]{1,0:T(8,128)S(1)} %get-tuple-element.177), channel_id=1, source_target_pairs={{0,4},{1,5},{2,6},{3,7},{4,0},{5,1},{6,2},{7,3},{8,12},{9,13},{10,... | collective-permute-start | bytes 589832 | tf_op jit(solution)/shard_map/ppermute | solution.py:164
  192.4 9.9 %collective-permute-start.33 = (f32[192,256]{1,0:T(8,128)S(1)}, f32[192,256]{1,0:T(8,128)S(1)}, u32[]{:S(2)}, u32[]{:S(2)}) collective-permute-start(f32[192,256]{1,0:T(8,128)S(1)} %get-tuple-element.176), channel_id=1, source_target_pairs={{0,12},{1,13},{2,14},{3,15},{4,8},{5,9},{6,10},{7,11},{8,4},{9,5},... | collective-permute-start | bytes 589832 | tf_op jit(solution)/shard_map/ppermute | solution.py:164
  193.0 9.3 %collective-permute-start.30 = (f32[768,128]{1,0:T(8,128)S(1)}, f32[768,128]{1,0:T(8,128)S(1)}, u32[]{:S(2)}, u32[]{:S(2)}) collective-permute-start(f32[768,128]{1,0:T(8,128)S(1)} %slice.137), channel_id=1, source_target_pairs={{0,1},{1,0},{2,3},{3,2},{4,5},{5,4},{6,7},{7,6},{8,9},{9,8},{10,11... | collective-permute-start | bytes 1179656 | tf_op jit(solution)/shard_map/ppermute | solution.py:164
  202.4 7.8 %collective-permute-start.34 = (f32[192,128]{1,0:T(8,128)S(1)}, f32[192,128]{1,0:T(8,128)S(1)}, u32[]{:S(2)}, u32[]{:S(2)}) collective-permute-start(f32[192,128]{1,0:T(8,128)S(1)} %get-tuple-element.178), channel_id=1, source_target_pairs={{0,8},{1,9},{2,10},{3,11},{4,12},{5,13},{6,14},{7,15},{8,0},{9,1},... | collective-permute-start | bytes 294920 | tf_op jit(solution)/shard_map/ppermute | solution.py:164
  204.4 5.8 %collective-permute-start.35 = (f32[192,128]{1,0:T(8,128)S(1)}, f32[192,128]{1,0:T(8,128)S(1)}, u32[]{:S(2)}, u32[]{:S(2)}) collective-permute-start(f32[192,128]{1,0:T(8,128)S(1)} %get-tuple-element.180), channel_id=1, source_target_pairs={{0,4},{1,5},{2,6},{3,7},{4,0},{5,1},{6,2},{7,3},{8,12},{9,13},{10,... | collective-permute-start | bytes 294920 | tf_op jit(solution)/shard_map/ppermute | solution.py:164
  205.2 5.1 %collective-permute-start.36 = (f32[192,128]{1,0:T(8,128)S(1)}, f32[192,128]{1,0:T(8,128)S(1)}, u32[]{:S(2)}, u32[]{:S(2)}) collective-permute-start(f32[192,128]{1,0:T(8,128)S(1)} %get-tuple-element.179), channel_id=1, source_target_pairs={{0,12},{1,13},{2,14},{3,15},{4,8},{5,9},{6,10},{7,11},{8,4},{9,5},... | collective-permute-start | bytes 294920 | tf_op jit(solution)/shard_map/ppermute | solution.py:164
  205.8 8.8 %collective-permute-start.38 = (f32[96,640]{1,0:T(8,128)S(1)}, f32[96,640]{1,0:T(8,128)S(1)}, u32[]{:S(2)}, u32[]{:S(2)}) collective-permute-start(f32[96,640]{1,0:T(8,128)S(1)} %slice.157), channel_id=1, source_target_pairs={{0,2},{1,3},{2,0},{3,1},{4,6},{5,7},{6,4},{7,5},{8,10},{9,11},{10,... | collective-permute-start | bytes 737288 | tf_op jit(solution)/shard_map/ppermute | solution.py:164
  208.2 6.4 %collective-permute-start.37 = (f32[192,256]{1,0:T(8,128)S(1)}, f32[192,256]{1,0:T(8,128)S(1)}, u32[]{:S(2)}, u32[]{:S(2)}) collective-permute-start(f32[192,256]{1,0:T(8,128)S(1)} %slice.147), channel_id=1, source_target_pairs={{0,8},{1,9},{2,10},{3,11},{4,12},{5,13},{6,14},{7,15},{8,0},{9,1},... | collective-permute-start | bytes 589832 | tf_op jit(solution)/shard_map/ppermute | solution.py:164
  214.6 1.6 copy-start.5
  214.6 7.2 %copy-start.8 = (f32[512]{0:T(512)S(1)}, f32[512]{0:T(512)}, u32[]{:S(2)}) copy-start(f32[512]{0:T(512)} %param.10) | copy-start | bytes 6148
  214.7 7.2 %collective-permute-start.39 = (f32[96,384]{1,0:T(8,128)S(1)}, f32[96,384]{1,0:T(8,128)S(1)}, u32[]{:S(2)}, u32[]{:S(2)}) collective-permute-start(f32[96,384]{1,0:T(8,128)S(1)} %slice.159), channel_id=1, source_target_pairs={{0,2},{1,3},{2,0},{3,1},{4,6},{5,7},{6,4},{7,5},{8,10},{9,11},{10,... | collective-permute-start | bytes 442376 | tf_op jit(solution)/shard_map/ppermute | solution.py:164
  222.1 0.7 copy-start.7

commit v3 on v2

--- a/solution.py
+++ b/solution.py
@@ -220,8 +220,10 @@
     last = step("core", last)
     third = sum_z(third)
     last, third, second, early = lax.optimization_barrier((last, third, second, early))
-    last = sum_z(last)
-    second = step("far", second)
+    width, split = 2 * cap, second.shape[1]
+    away = swap(jnp.concatenate([second[width:], last[width : 2 * width]], axis=1), 8)
+    second = second[:width] + away[:, :split]
+    last = last[:width] + away[:, split:] + swap(last[2 * width : 3 * width], 4) + swap(last[3 * width :], 12)
     early = step("y", jnp.concatenate([early, third], axis=1))
     last, second, early = lax.optimization_barrier((last, second, early))
     parts = [early, step("y", jnp.concatenate([second, last], axis=1))]

time: 226 us -> 227 us (level)
  waiting for transfers between devices: 56.7 us -> 61.5 us
  starting transfers between devices: 81.8 us -> 79.4 us
    ppermute x19 -> x18, waiting for transfers between devices: 19.6 us -> 24.5 us  [swap(): return lax.ppermute(part, 'vslab', [(i, i ^ bits) for i in range(owners)])]
    ppermute x19 -> x18, starting transfers between devices: 56 us -> 53.5 us  [swap(): return lax.ppermute(part, 'vslab', [(i, i ^ bits) for i in range(owners)])]
  transfers between devices with their start and end apart: 40 -> 39, of which waited for: 17 -> 20; matrix products, arithmetic and copies ran while one was open for 2% -> 2% of each run, Pallas kernels for 26% -> 26%
where the time goes in v3:
time: 227 us; the launch traced here: 226 us
  starting transfers between devices  79.4 us (35%)
  waiting for transfers between devices  61.5 us (27%)
  Pallas kernels  59.2 us (26%)
  local copies, waits for them, and re-layouts  16.6 us (7%)
  between operations  5.99 us (3%)
  other arithmetic  3.36 us (1%)
    ppermute x18, starting transfers between devices, swap(): return lax.ppermute(part, 'vslab', [(i, i ^ bits) for i in range(owners)])  53.5 us
    pallas_call x24, Pallas kernels, product(): pl.pallas_call(product_kernel, grid=(steps,), in_specs=[pl.BlockSpec((til...  49 us
    ppermute x21, waiting for transfers between devices, on_device(): lax.ppermute(held[p, offset], 'blk', link_pairs(STEPS[link]))  37 us
    ppermute x21, starting transfers between devices, on_device(): lax.ppermute(held[p, offset], 'blk', link_pairs(STEPS[link]))  25.9 us
    ppermute x18, waiting for transfers between devices, swap(): return lax.ppermute(part, 'vslab', [(i, i ^ bits) for i in range(owners)])  24.5 us
    unnamed x24, local copies, waits for them, and re-layouts  11.4 us
    pallas_call x5, Pallas kernels, pack(): pl.pallas_call(pack_kernel, grid=(4,), in_specs=[pl.BlockSpec((tile, hot....  10.1 us
  transfers between devices with their start and end apart: 39, of which 20 were waited for; matrix products, arithmetic and copies ran while one was open for 2% of the time, Pallas kernels for 26%

profile of v3, /device:TPU:1, one launch (start us, length us, event | category | flops | bytes accessed | tf_op | source)
XLA Modules:
  0.0 226.1 jit_solution(14941476281754223434)
XLA Ops:
  0.0 2.3 %slice.161.t_ref = f32[2112,128]{1,0:T(8,128)} slice(f32[6400,128]{1,0:T(8,128)} %bitcast.38), slice={[0:2112], [0:128]} | slice | bytes 2162688 | tf_op jit(solution)/shard_map/slice | solution.py:141
  2.3 2.0 collective-permute-start
  5.6 1.5 collective-permute-start.2
  7.1 1.7 fusion.21
  8.8 5.1 %copy-done = f32[8,800,512]{2,1,0:T(8,128)S(1)} copy-done((f32[8,800,512]{2,1,0:T(8,128)S(1)}, f32[8,800,512]{2,1,0:T(8,128)}, u32[]{:S(2)}) %copy-start) | copy-done | bytes 13107224
  13.9 3.5 %product.24 = f32[128,512]{1,0:T(8,128)S(1)} custom-call(f32[2112,128]{1,0:T(8,128)} %slice.161.t_ref, f32[6400,512]{1,0:T(8,128)S(1)} %bitcast.14), custom_call_target="tpu_custom_call" | custom-call | flops 1 | bytes 1 | tf_op jit(solution)/shard_map/product/pallas_call | solution.py:89
  17.5 1.6 product.25
  19.2 1.6 product.26
  21.7 1.9 pack.5
  23.6 5.4 %collective-permute-done.t_ref = f32[2112,128]{1,0:T(8,128)} collective-permute-done((f32[2112,128]{1,0:T(8,128)}, f32[2112,128]{1,0:T(8,128)}, u32[]{:S(2)}, u32[]{:S(2)}) %collective-permute-start) | collective-permute-done | bytes 1081376 | tf_op jit(solution)/shard_map/ppermute | solution.py:198
  31.6 2.6 %collective-permute-start.4 = (f32[2144,128]{1,0:T(8,128)S(1)}, f32[2144,128]{1,0:T(8,128)S(1)}, u32[]{:S(2)}, u32[]{:S(2)}) collective-permute-start(f32[2144,128]{1,0:T(8,128)S(1)} %copy-done.4), channel_id=1, source_target_pairs={{0,48},{16,0},{32,16},{48,32},{64,112},{80,64},{96,80},{112,96},{1... | collective-permute-start | bytes 3293192 | tf_op jit(solution)/shard_map/ppermute | solution.py:198
  34.2 3.1 %collective-permute-start.6 = (f32[768,128]{1,0:T(8,128)S(1)}, f32[768,128]{1,0:T(8,128)S(1)}, u32[]{:S(2)}, u32[]{:S(2)}) collective-permute-start(f32[768,128]{1,0:T(8,128)S(1)} %slice.125), channel_id=1, source_target_pairs={{0,1},{1,0},{2,3},{3,2},{4,5},{5,4},{6,7},{7,6},{8,9},{9,8},{10,11... | collective-permute-start | bytes 1179656 | tf_op jit(solution)/shard_map/ppermute | solution.py:164
  37.3 4.7 %copy-done.1 = f32[8,800,512]{2,1,0:T(8,128)S(1)} copy-done((f32[8,800,512]{2,1,0:T(8,128)S(1)}, f32[8,800,512]{2,1,0:T(8,128)}, u32[]{:S(2)}) %copy-start.1) | copy-done | bytes 13107224
  42.0 4.1 %product.27 = f32[128,512]{1,0:T(8,128)S(1)} custom-call(f32[2112,128]{1,0:T(8,128)} %collective-permute-done.t_ref, f32[6400,512]{1,0:T(8,128)S(1)} %bitcast.17), custom_call_target="tpu_custom_call" | custom-call | flops 1 | bytes 1 | tf_op jit(solution)/shard_map/product/pallas_call | solution.py:89
  47.1 3.5 %product.28 = f32[128,512]{1,0:T(8,128)S(1)} custom-call(f32[2112,128]{1,0:T(8,128)} %collective-permute-done.1.t_ref, f32[6400,512]{1,0:T(8,128)S(1)} %bitcast.18), custom_call_target="tpu_custom_call" | custom-call | flops 1 | bytes 1 | tf_op jit(solution)/shard_map/product/pallas_call | solution.py:89
  50.6 3.6 %product.29 = f32[128,512]{1,0:T(8,128)S(1)} custom-call(f32[2112,128]{1,0:T(8,128)} %collective-permute-done.2.t_ref, f32[6400,512]{1,0:T(8,128)S(1)} %bitcast.19), custom_call_target="tpu_custom_call" | custom-call | flops 1 | bytes 1 | tf_op jit(solution)/shard_map/product/pallas_call | solution.py:89
  55.7 2.7 %collective-permute-start.8 = (f32[2144,128]{1,0:T(8,128)S(1)}, f32[2144,128]{1,0:T(8,128)S(1)}, u32[]{:S(2)}, u32[]{:S(2)}) collective-permute-start(f32[2144,128]{1,0:T(8,128)S(1)} %get-tuple-element.95.t_ref), channel_id=1, source_target_pairs={{0,48},{16,0},{32,16},{48,32},{64,112},{80,64},{96,80},{112,96},{1... | collective-permute-start | bytes 3293192 | tf_op jit(solution)/shard_map/ppermute | solution.py:198
  59.0 1.7 collective-permute-start.10
  60.7 1.6 product.31
  62.3 1.6 product.32
  63.9 1.6 product.30
  65.7 13.6 %collective-permute-done.7.t_ref = f32[2144,128]{1,0:T(8,128)S(1)} collective-permute-done((f32[2144,128]{1,0:T(8,128)S(1)}, f32[2144,128]{1,0:T(8,128)S(1)}, u32[]{:S(2)}, u32[]{:S(2)}) %collective-permute-start.7) | collective-permute-done | bytes 1097760 | tf_op jit(solution)/shard_map/ppermute | solution.py:198
  80.2 2.7 %collective-permute-start.12 = (f32[2144,128]{1,0:T(8,128)S(1)}, f32[2144,128]{1,0:T(8,128)S(1)}, u32[]{:S(2)}, u32[]{:S(2)}) collective-permute-start(f32[2144,128]{1,0:T(8,128)S(1)} %collective-permute-done.5.t_ref), channel_id=1, source_target_pairs={{0,48},{16,0},{32,16},{48,32},{64,112},{80,64},{96,80},{112,96},{1... | collective-permute-start | bytes 3293192 | tf_op jit(solution)/shard_map/ppermute | solution.py:198
  83.7 1.6 product.34
  85.3 1.6 product.35
  86.9 3.9 %collective-permute-start.14 = (f32[192,128]{1,0:T(8,128)S(1)}, f32[192,128]{1,0:T(8,128)S(1)}, u32[]{:S(2)}, u32[]{:S(2)}) collective-permute-start(f32[192,128]{1,0:T(8,128)S(1)} %slice.129), channel_id=1, source_target_pairs={{0,8},{1,9},{2,10},{3,11},{4,12},{5,13},{6,14},{7,15},{8,0},{9,1},... | collective-permute-start | bytes 294920 | tf_op jit(solution)/shard_map/ppermute | solution.py:164
  90.9 1.6 product.33
  92.5 2.1 pack.6
  94.7 8.4 %collective-permute-done.13.t_ref = f32[2112,128]{1,0:T(8,128)S(1)} collective-permute-done((f32[2112,128]{1,0:T(8,128)}, f32[2112,128]{1,0:T(8,128)S(1)}, u32[]{:S(2)}, u32[]{:S(2)}) %collective-permute-start.13) | collective-permute-done | bytes 1081376 | tf_op jit(solution)/shard_map/ppermute | solution.py:198
  103.0 1.6 collective-permute-start.16
  105.8 8.0 %collective-permute-start.18 = (f32[768,256]{1,0:T(8,128)S(1)}, f32[768,256]{1,0:T(8,128)S(1)}, u32[]{:S(2)}, u32[]{:S(2)}) collective-permute-start(f32[768,256]{1,0:T(8,128)S(1)} %slice.131), channel_id=1, source_target_pairs={{0,1},{1,0},{2,3},{3,2},{4,5},{5,4},{6,7},{7,6},{8,9},{9,8},{10,11... | collective-permute-start | bytes 2359304 | tf_op jit(solution)/shard_map/ppermute | solution.py:164
  113.9 1.6 product.36
  115.5 1.6 product.37
  117.1 2.2 product.38
  119.4 2.1 pack.7
  121.7 3.2 %collective-permute-done.15.t_ref = f32[2112,128]{1,0:T(8,128)S(1)} collective-permute-done((f32[2112,128]{1,0:T(8,128)}, f32[2112,128]{1,0:T(8,128)S(1)}, u32[]{:S(2)}, u32[]{:S(2)}) %collective-permute-start.15) | collective-permute-done | bytes 1081376 | tf_op jit(solution)/shard_map/ppermute | solution.py:198
  125.6 1.8 collective-permute-start.20
  128.5 9.7 %collective-permute-start.23 = (f32[768,256]{1,0:T(8,128)S(1)}, f32[768,256]{1,0:T(8,128)S(1)}, u32[]{:S(2)}, u32[]{:S(2)}) collective-permute-start(f32[768,256]{1,0:T(8,128)S(1)} %slice.135), channel_id=1, source_target_pairs={{0,1},{1,0},{2,3},{3,2},{4,5},{5,4},{6,7},{7,6},{8,9},{9,8},{10,11... | collective-permute-start | bytes 2359304 | tf_op jit(solution)/shard_map/ppermute | solution.py:164
  138.3 1.7 collective-permute-start.22
  140.0 2.2 product.39
  142.2 1.6 product.40
  143.8 1.6 product.41
  145.5 3.9 %collective-permute-done.22 = f32[384,256]{1,0:T(8,128)S(1)} collective-permute-done((f32[384,256]{1,0:T(8,128)S(1)}, f32[384,256]{1,0:T(8,128)S(1)}, u32[]{:S(2)}, u32[]{:S(2)}) %collective-permute-start.22) | collective-permute-done | bytes 393248 | tf_op jit(solution)/shard_map/ppermute | solution.py:164
  150.6 2.7 %collective-permute-start.25 = (f32[2112,128]{1,0:T(8,128)S(1)}, f32[2112,128]{1,0:T(8,128)S(1)}, u32[]{:S(2)}, u32[]{:S(2)}) collective-permute-start(f32[2112,128]{1,0:T(8,128)S(1)} %collective-permute-done.13.t_ref), channel_id=1, source_target_pairs={{0,48},{16,0},{32,16},{48,32},{64,112},{80,64},{96,80},{112,96},{1... | collective-permute-start | bytes 3244040 | tf_op jit(solution)/shard_map/ppermute | solution.py:198
  153.3 2.2 product.43
  155.5 1.6 product.44
  158.6 3.6 %collective-permute-start.27 = (f32[192,256]{1,0:T(8,128)S(1)}, f32[192,256]{1,0:T(8,128)S(1)}, u32[]{:S(2)}, u32[]{:S(2)}) collective-permute-start(f32[192,256]{1,0:T(8,128)S(1)} %slice.137), channel_id=1, source_target_pairs={{0,8},{1,9},{2,10},{3,11},{4,12},{5,13},{6,14},{7,15},{8,0},{9,1},... | collective-permute-start | bytes 589832 | tf_op jit(solution)/shard_map/ppermute | solution.py:164
  162.3 1.6 product.42
  164.0 2.1 pack.8
  166.1 3.1 %collective-permute-done.27 = f32[192,256]{1,0:T(8,128)S(1)} collective-permute-done((f32[192,256]{1,0:T(8,128)S(1)}, f32[192,256]{1,0:T(8,128)S(1)}, u32[]{:S(2)}, u32[]{:S(2)}) %collective-permute-start.27) | collective-permute-done | bytes 196640 | tf_op jit(solution)/shard_map/ppermute | solution.py:164
  169.3 2.4 %collective-permute-done.24.t_ref = f32[2144,128]{1,0:T(8,128)S(1)} collective-permute-done((f32[2144,128]{1,0:T(8,128)S(1)}, f32[2144,128]{1,0:T(8,128)S(1)}, u32[]{:S(2)}, u32[]{:S(2)}) %collective-permute-start.24) | collective-permute-done | bytes 1097760 | tf_op jit(solution)/shard_map/ppermute | solution.py:198
  172.5 9.5 %collective-permute-start.29 = (f32[768,256]{1,0:T(8,128)S(1)}, f32[768,256]{1,0:T(8,128)S(1)}, u32[]{:S(2)}, u32[]{:S(2)}) collective-permute-start(f32[768,256]{1,0:T(8,128)S(1)} %slice.141), channel_id=1, source_target_pairs={{0,1},{1,0},{2,3},{3,2},{4,5},{5,4},{6,7},{7,6},{8,9},{9,8},{10,11... | collective-permute-start | bytes 2359304 | tf_op jit(solution)/shard_map/ppermute | solution.py:164
  182.0 1.6 product.45
  183.6 2.2 product.46
  185.8 1.6 product.47
  187.5 1.9 pack.9
  189.6 2.0 collective-permute-start.31
  194.0 3.7 %collective-permute-done.31 = f32[192,256]{1,0:T(8,128)S(1)} collective-permute-done((f32[192,256]{1,0:T(8,128)S(1)}, f32[192,256]{1,0:T(8,128)S(1)}, u32[]{:S(2)}, u32[]{:S(2)}) %collective-permute-start.31) | collective-permute-done | bytes 196640 | tf_op jit(solution)/shard_map/ppermute | solution.py:164
  197.7 4.0 %collective-permute-done.32 = f32[192,256]{1,0:T(8,128)S(1)} collective-permute-done((f32[192,256]{1,0:T(8,128)S(1)}, f32[192,256]{1,0:T(8,128)S(1)}, u32[]{:S(2)}, u32[]{:S(2)}) %collective-permute-start.32) | collective-permute-done | bytes 196640 | tf_op jit(solution)/shard_map/ppermute | solution.py:164
  202.4 2.4 %collective-permute-start.37 = (f32[96,640]{1,0:T(8,128)S(1)}, f32[96,640]{1,0:T(8,128)S(1)}, u32[]{:S(2)}, u32[]{:S(2)}) collective-permute-start(f32[96,640]{1,0:T(8,128)S(1)} %slice.167), channel_id=1, source_target_pairs={{0,2},{1,3},{2,0},{3,1},{4,6},{5,7},{6,4},{7,5},{8,10},{9,11},{10,... | collective-permute-start | bytes 737288 | tf_op jit(solution)/shard_map/ppermute | solution.py:164
  204.9 2.1 collective-permute-start.34
  208.2 2.8 %collective-permute-done.37 = f32[96,640]{1,0:T(8,128)S(1)} collective-permute-done((f32[96,640]{1,0:T(8,128)S(1)}, f32[96,640]{1,0:T(8,128)S(1)}, u32[]{:S(2)}, u32[]{:S(2)}) %collective-permute-start.37) | collective-permute-done | bytes 245792 | tf_op jit(solution)/shard_map/ppermute | solution.py:164
  211.1 3.1 %collective-permute-done.34 = f32[192,384]{1,0:T(8,128)S(1)} collective-permute-done((f32[192,384]{1,0:T(8,128)S(1)}, f32[192,384]{1,0:T(8,128)S(1)}, u32[]{:S(2)}, u32[]{:S(2)}) %collective-permute-start.34) | collective-permute-done | bytes 294944 | tf_op jit(solution)/shard_map/ppermute | solution.py:164
  214.3 1.8 collective-permute-done.35
  (138 shorter events, 26.1 us)
Async XLA Ops:
  2.3 26.8 %collective-permute-start = (f32[2112,128]{1,0:T(8,128)}, f32[2112,128]{1,0:T(8,128)}, u32[]{:S(2)}, u32[]{:S(2)}) collective-permute-start(f32[2112,128]{1,0:T(8,128)} %slice.161.t_ref), channel_id=1, source_target_pairs={{0,16},{16,32},{32,48},{48,0},{64,80},{80,96},{96,112},{112,64},{1... | collective-permute-start | bytes 3244040 | tf_op jit(solution)/shard_map/ppermute | solution.py:198
  4.3 24.7 %collective-permute-start.1 = (f32[2112,128]{1,0:T(8,128)}, f32[2112,128]{1,0:T(8,128)}, u32[]{:S(2)}, u32[]{:S(2)}) collective-permute-start(f32[2112,128]{1,0:T(8,128)} %slice.161.t_ref), channel_id=1, source_target_pairs={{0,48},{16,0},{32,16},{48,32},{64,112},{80,64},{96,80},{112,96},{1... | collective-permute-start | bytes 3244040 | tf_op jit(solution)/shard_map/ppermute | solution.py:198
  5.6 24.4 %collective-permute-start.2 = (f32[2112,128]{1,0:T(8,128)}, f32[2112,128]{1,0:T(8,128)}, u32[]{:S(2)}, u32[]{:S(2)}) collective-permute-start(f32[2112,128]{1,0:T(8,128)} %slice.161.t_ref), channel_id=1, source_target_pairs={{0,64},{16,80},{32,96},{48,112},{64,0},{80,16},{96,32},{112,48},{1... | collective-permute-start | bytes 3244040 | tf_op jit(solution)/shard_map/ppermute | solution.py:198
  8.8 8.7 %copy-start.3 = (f32[2144,128]{1,0:T(8,128)}, f32[2144,128]{1,0:T(8,128)S(1)}, u32[]{:S(2)}) copy-start(f32[2144,128]{1,0:T(8,128)S(1)} %get-tuple-element.94.t_ref) | copy-start | bytes 3293188
  8.8 5.1 %copy-start = (f32[8,800,512]{2,1,0:T(8,128)S(1)}, f32[8,800,512]{2,1,0:T(8,128)}, u32[]{:S(2)}) copy-start(f32[8,800,512]{2,1,0:T(8,128)} %param.9) | copy-start | bytes 39321604
  19.1 1.7 copy-start.10
  19.1 1.8 copy-start.6
  19.2 1.8 copy-start.9
  21.7 9.9 %copy-start.4 = (f32[2144,128]{1,0:T(8,128)S(1)}, f32[2144,128]{1,0:T(8,128)}, u32[]{:S(2)}) copy-start(f32[2144,128]{1,0:T(8,128)} %copy-done.3) | copy-start | bytes 3293188
  30.0 24.7 %collective-permute-start.3 = (f32[2144,128]{1,0:T(8,128)S(1)}, f32[2144,128]{1,0:T(8,128)S(1)}, u32[]{:S(2)}, u32[]{:S(2)}) collective-permute-start(f32[2144,128]{1,0:T(8,128)S(1)} %get-tuple-element.95.t_ref), channel_id=1, source_target_pairs={{0,16},{16,32},{32,48},{48,0},{64,80},{80,96},{96,112},{112,64},{1... | collective-permute-start | bytes 3293192 | tf_op jit(solution)/shard_map/ppermute | solution.py:198
  30.3 24.5 %collective-permute-start.5 = (f32[2144,128]{1,0:T(8,128)S(1)}, f32[2144,128]{1,0:T(8,128)S(1)}, u32[]{:S(2)}, u32[]{:S(2)}) collective-permute-start(f32[2144,128]{1,0:T(8,128)S(1)} %get-tuple-element.95.t_ref), channel_id=1, source_target_pairs={{0,64},{16,80},{32,96},{48,112},{64,0},{80,16},{96,32},{112,48},{1... | collective-permute-start | bytes 3293192 | tf_op jit(solution)/shard_map/ppermute | solution.py:198
  31.6 23.4 %collective-permute-start.4 = (f32[2144,128]{1,0:T(8,128)S(1)}, f32[2144,128]{1,0:T(8,128)S(1)}, u32[]{:S(2)}, u32[]{:S(2)}) collective-permute-start(f32[2144,128]{1,0:T(8,128)S(1)} %copy-done.4), channel_id=1, source_target_pairs={{0,48},{16,0},{32,16},{48,32},{64,112},{80,64},{96,80},{112,96},{1... | collective-permute-start | bytes 3293192 | tf_op jit(solution)/shard_map/ppermute | solution.py:198
  34.2 20.0 %collective-permute-start.6 = (f32[768,128]{1,0:T(8,128)S(1)}, f32[768,128]{1,0:T(8,128)S(1)}, u32[]{:S(2)}, u32[]{:S(2)}) collective-permute-start(f32[768,128]{1,0:T(8,128)S(1)} %slice.125), channel_id=1, source_target_pairs={{0,1},{1,0},{2,3},{3,2},{4,5},{5,4},{6,7},{7,6},{8,9},{9,8},{10,11... | collective-permute-start | bytes 1179656 | tf_op jit(solution)/shard_map/ppermute | solution.py:164
  37.3 4.7 %copy-start.1 = (f32[8,800,512]{2,1,0:T(8,128)S(1)}, f32[8,800,512]{2,1,0:T(8,128)}, u32[]{:S(2)}) copy-start(f32[8,800,512]{2,1,0:T(8,128)} %param.9) | copy-start | bytes 39321604
  42.0 5.0 %copy-start.2 = (f32[8,800,512]{2,1,0:T(8,128)S(1)}, f32[8,800,512]{2,1,0:T(8,128)}, u32[]{:S(2)}) copy-start(f32[8,800,512]{2,1,0:T(8,128)} %param.9) | copy-start | bytes 39321604
  55.0 24.3 %collective-permute-start.7 = (f32[2144,128]{1,0:T(8,128)S(1)}, f32[2144,128]{1,0:T(8,128)S(1)}, u32[]{:S(2)}, u32[]{:S(2)}) collective-permute-start(f32[2144,128]{1,0:T(8,128)S(1)} %copy-done.4), channel_id=1, source_target_pairs={{0,16},{16,32},{32,48},{48,0},{64,80},{80,96},{96,112},{112,64},{1... | collective-permute-start | bytes 3293192 | tf_op jit(solution)/shard_map/ppermute | solution.py:198
  55.7 23.6 %collective-permute-start.8 = (f32[2144,128]{1,0:T(8,128)S(1)}, f32[2144,128]{1,0:T(8,128)S(1)}, u32[]{:S(2)}, u32[]{:S(2)}) collective-permute-start(f32[2144,128]{1,0:T(8,128)S(1)} %get-tuple-element.95.t_ref), channel_id=1, source_target_pairs={{0,48},{16,0},{32,16},{48,32},{64,112},{80,64},{96,80},{112,96},{1... | collective-permute-start | bytes 3293192 | tf_op jit(solution)/shard_map/ppermute | solution.py:198
  58.4 21.8 %collective-permute-start.9 = (f32[2144,128]{1,0:T(8,128)S(1)}, f32[2144,128]{1,0:T(8,128)S(1)}, u32[]{:S(2)}, u32[]{:S(2)}) collective-permute-start(f32[2144,128]{1,0:T(8,128)S(1)} %collective-permute-done.4.t_ref), channel_id=1, source_target_pairs={{0,64},{16,80},{32,96},{48,112},{64,0},{80,16},{96,32},{112,48},{1... | collective-permute-start | bytes 3293192 | tf_op jit(solution)/shard_map/ppermute | solution.py:198
  59.0 6.7 %collective-permute-start.10 = (f32[384,128]{1,0:T(8,128)S(1)}, f32[384,128]{1,0:T(8,128)S(1)}, u32[]{:S(2)}, u32[]{:S(2)}) collective-permute-start(f32[384,128]{1,0:T(8,128)S(1)} %slice.127), channel_id=1, source_target_pairs={{0,4},{1,5},{2,6},{3,7},{4,0},{5,1},{6,2},{7,3},{8,12},{9,13},{10,... | collective-permute-start | bytes 589832 | tf_op jit(solution)/shard_map/ppermute | solution.py:164
  80.2 22.8 %collective-permute-start.11 = (f32[2144,128]{1,0:T(8,128)S(1)}, f32[2144,128]{1,0:T(8,128)S(1)}, u32[]{:S(2)}, u32[]{:S(2)}) collective-permute-start(f32[2144,128]{1,0:T(8,128)S(1)} %collective-permute-done.9.t_ref), channel_id=1, source_target_pairs={{0,16},{16,32},{32,48},{48,0},{64,80},{80,96},{96,112},{112,64},{1... | collective-permute-start | bytes 3293192 | tf_op jit(solution)/shard_map/ppermute | solution.py:198
  80.2 22.8 %collective-permute-start.12 = (f32[2144,128]{1,0:T(8,128)S(1)}, f32[2144,128]{1,0:T(8,128)S(1)}, u32[]{:S(2)}, u32[]{:S(2)}) collective-permute-start(f32[2144,128]{1,0:T(8,128)S(1)} %collective-permute-done.5.t_ref), channel_id=1, source_target_pairs={{0,48},{16,0},{32,16},{48,32},{64,112},{80,64},{96,80},{112,96},{1... | collective-permute-start | bytes 3293192 | tf_op jit(solution)/shard_map/ppermute | solution.py:198
  82.9 20.2 %collective-permute-start.13 = (f32[2112,128]{1,0:T(8,128)}, f32[2112,128]{1,0:T(8,128)S(1)}, u32[]{:S(2)}, u32[]{:S(2)}) collective-permute-start(f32[2112,128]{1,0:T(8,128)} %collective-permute-done.1.t_ref), channel_id=1, source_target_pairs={{0,64},{16,80},{32,96},{48,112},{64,0},{80,16},{96,32},{112,48},{1... | collective-permute-start | bytes 3244040 | tf_op jit(solution)/shard_map/ppermute | solution.py:198
  86.9 7.7 %collective-permute-start.14 = (f32[192,128]{1,0:T(8,128)S(1)}, f32[192,128]{1,0:T(8,128)S(1)}, u32[]{:S(2)}, u32[]{:S(2)}) collective-permute-start(f32[192,128]{1,0:T(8,128)S(1)} %slice.129), channel_id=1, source_target_pairs={{0,8},{1,9},{2,10},{3,11},{4,12},{5,13},{6,14},{7,15},{8,0},{9,1},... | collective-permute-start | bytes 294920 | tf_op jit(solution)/shard_map/ppermute | solution.py:164
  103.0 21.8 %collective-permute-start.16 = (f32[2144,128]{1,0:T(8,128)S(1)}, f32[2144,128]{1,0:T(8,128)S(1)}, u32[]{:S(2)}, u32[]{:S(2)}) collective-permute-start(f32[2144,128]{1,0:T(8,128)S(1)} %collective-permute-done.8.t_ref), channel_id=1, source_target_pairs={{0,48},{16,0},{32,16},{48,32},{64,112},{80,64},{96,80},{112,96},{1... | collective-permute-start | bytes 3293192 | tf_op jit(solution)/shard_map/ppermute | solution.py:198
  104.7 20.9 %collective-permute-start.17 = (f32[2144,128]{1,0:T(8,128)S(1)}, f32[2144,128]{1,0:T(8,128)S(1)}, u32[]{:S(2)}, u32[]{:S(2)}) collective-permute-start(f32[2144,128]{1,0:T(8,128)S(1)} %collective-permute-done.7.t_ref), channel_id=1, source_target_pairs={{0,64},{16,80},{32,96},{48,112},{64,0},{80,16},{96,32},{112,48},{1... | collective-permute-start | bytes 3293192 | tf_op jit(solution)/shard_map/ppermute | solution.py:198
  105.8 19.1 %collective-permute-start.15 = (f32[2112,128]{1,0:T(8,128)}, f32[2112,128]{1,0:T(8,128)S(1)}, u32[]{:S(2)}, u32[]{:S(2)}) collective-permute-start(f32[2112,128]{1,0:T(8,128)} %collective-permute-done.2.t_ref), channel_id=1, source_target_pairs={{0,16},{16,32},{32,48},{48,0},{64,80},{80,96},{96,112},{112,64},{1... | collective-permute-start | bytes 3244040 | tf_op jit(solution)/shard_map/ppermute | solution.py:198
  105.8 15.7 %collective-permute-start.18 = (f32[768,256]{1,0:T(8,128)S(1)}, f32[768,256]{1,0:T(8,128)S(1)}, u32[]{:S(2)}, u32[]{:S(2)}) collective-permute-start(f32[768,256]{1,0:T(8,128)S(1)} %slice.131), channel_id=1, source_target_pairs={{0,1},{1,0},{2,3},{3,2},{4,5},{5,4},{6,7},{7,6},{8,9},{9,8},{10,11... | collective-permute-start | bytes 2359304 | tf_op jit(solution)/shard_map/ppermute | solution.py:164
  125.6 24.0 %collective-permute-start.20 = (f32[2144,128]{1,0:T(8,128)S(1)}, f32[2144,128]{1,0:T(8,128)S(1)}, u32[]{:S(2)}, u32[]{:S(2)}) collective-permute-start(f32[2144,128]{1,0:T(8,128)S(1)} %collective-permute-done.4.t_ref), channel_id=1, source_target_pairs={{0,48},{16,0},{32,16},{48,32},{64,112},{80,64},{96,80},{112,96},{1... | collective-permute-start | bytes 3293192 | tf_op jit(solution)/shard_map/ppermute | solution.py:198
  127.3 22.2 %collective-permute-start.21 = (f32[2144,128]{1,0:T(8,128)S(1)}, f32[2144,128]{1,0:T(8,128)S(1)}, u32[]{:S(2)}, u32[]{:S(2)}) collective-permute-start(f32[2144,128]{1,0:T(8,128)S(1)} %collective-permute-done.3.t_ref), channel_id=1, source_target_pairs={{0,64},{16,80},{32,96},{48,112},{64,0},{80,16},{96,32},{112,48},{1... | collective-permute-start | bytes 3293192 | tf_op jit(solution)/shard_map/ppermute | solution.py:198
  128.5 21.1 %collective-permute-start.19 = (f32[2112,128]{1,0:T(8,128)}, f32[2112,128]{1,0:T(8,128)S(1)}, u32[]{:S(2)}, u32[]{:S(2)}) collective-permute-start(f32[2112,128]{1,0:T(8,128)} %collective-permute-done.t_ref), channel_id=1, source_target_pairs={{0,16},{16,32},{32,48},{48,0},{64,80},{80,96},{96,112},{112,64},{1... | collective-permute-start | bytes 3244040 | tf_op jit(solution)/shard_map/ppermute | solution.py:198
  128.5 20.9 %collective-permute-start.23 = (f32[768,256]{1,0:T(8,128)S(1)}, f32[768,256]{1,0:T(8,128)S(1)}, u32[]{:S(2)}, u32[]{:S(2)}) collective-permute-start(f32[768,256]{1,0:T(8,128)S(1)} %slice.135), channel_id=1, source_target_pairs={{0,1},{1,0},{2,3},{3,2},{4,5},{5,4},{6,7},{7,6},{8,9},{9,8},{10,11... | collective-permute-start | bytes 2359304 | tf_op jit(solution)/shard_map/ppermute | solution.py:164
  138.3 11.1 %collective-permute-start.22 = (f32[384,256]{1,0:T(8,128)S(1)}, f32[384,256]{1,0:T(8,128)S(1)}, u32[]{:S(2)}, u32[]{:S(2)}) collective-permute-start(f32[384,256]{1,0:T(8,128)S(1)} %slice.133), channel_id=1, source_target_pairs={{0,4},{1,5},{2,6},{3,7},{4,0},{5,1},{6,2},{7,3},{8,12},{9,13},{10,... | collective-permute-start | bytes 1179656 | tf_op jit(solution)/shard_map/ppermute | solution.py:164
  149.6 22.1 %collective-permute-start.24 = (f32[2144,128]{1,0:T(8,128)S(1)}, f32[2144,128]{1,0:T(8,128)S(1)}, u32[]{:S(2)}, u32[]{:S(2)}) collective-permute-start(f32[2144,128]{1,0:T(8,128)S(1)} %collective-permute-done.17.t_ref), channel_id=1, source_target_pairs={{0,16},{16,32},{32,48},{48,0},{64,80},{80,96},{96,112},{112,64},{1... | collective-permute-start | bytes 3293192 | tf_op jit(solution)/shard_map/ppermute | solution.py:198
  149.7 22.7 %collective-permute-start.26 = (f32[2144,128]{1,0:T(8,128)S(1)}, f32[2144,128]{1,0:T(8,128)S(1)}, u32[]{:S(2)}, u32[]{:S(2)}) collective-permute-start(f32[2144,128]{1,0:T(8,128)S(1)} %collective-permute-done.16.t_ref), channel_id=1, source_target_pairs={{0,64},{16,80},{32,96},{48,112},{64,0},{80,16},{96,32},{112,48},{1... | collective-permute-start | bytes 3293192 | tf_op jit(solution)/shard_map/ppermute | solution.py:198
  150.6 18.6 %collective-permute-start.25 = (f32[2112,128]{1,0:T(8,128)S(1)}, f32[2112,128]{1,0:T(8,128)S(1)}, u32[]{:S(2)}, u32[]{:S(2)}) collective-permute-start(f32[2112,128]{1,0:T(8,128)S(1)} %collective-permute-done.13.t_ref), channel_id=1, source_target_pairs={{0,48},{16,0},{32,16},{48,32},{64,112},{80,64},{96,80},{112,96},{1... | collective-permute-start | bytes 3244040 | tf_op jit(solution)/shard_map/ppermute | solution.py:198
  157.2 12.1 %collective-permute-start.28 = (f32[384,256]{1,0:T(8,128)S(1)}, f32[384,256]{1,0:T(8,128)S(1)}, u32[]{:S(2)}, u32[]{:S(2)}) collective-permute-start(f32[384,256]{1,0:T(8,128)S(1)} %slice.139), channel_id=1, source_target_pairs={{0,4},{1,5},{2,6},{3,7},{4,0},{5,1},{6,2},{7,3},{8,12},{9,13},{10,... | collective-permute-start | bytes 1179656 | tf_op jit(solution)/shard_map/ppermute | solution.py:164
  158.6 10.6 %collective-permute-start.27 = (f32[192,256]{1,0:T(8,128)S(1)}, f32[192,256]{1,0:T(8,128)S(1)}, u32[]{:S(2)}, u32[]{:S(2)}) collective-permute-start(f32[192,256]{1,0:T(8,128)S(1)} %slice.137), channel_id=1, source_target_pairs={{0,8},{1,9},{2,10},{3,11},{4,12},{5,13},{6,14},{7,15},{8,0},{9,1},... | collective-permute-start | bytes 589832 | tf_op jit(solution)/shard_map/ppermute | solution.py:164
  172.5 17.0 %collective-permute-start.29 = (f32[768,256]{1,0:T(8,128)S(1)}, f32[768,256]{1,0:T(8,128)S(1)}, u32[]{:S(2)}, u32[]{:S(2)}) collective-permute-start(f32[768,256]{1,0:T(8,128)S(1)} %slice.141), channel_id=1, source_target_pairs={{0,1},{1,0},{2,3},{3,2},{4,5},{5,4},{6,7},{7,6},{8,9},{9,8},{10,11... | collective-permute-start | bytes 2359304 | tf_op jit(solution)/shard_map/ppermute | solution.py:164
  189.6 8.1 %collective-permute-start.31 = (f32[192,256]{1,0:T(8,128)S(1)}, f32[192,256]{1,0:T(8,128)S(1)}, u32[]{:S(2)}, u32[]{:S(2)}) collective-permute-start(f32[192,256]{1,0:T(8,128)S(1)} %get-tuple-element.175), channel_id=1, source_target_pairs={{0,8},{1,9},{2,10},{3,11},{4,12},{5,13},{6,14},{7,15},{8,0},{9,1},... | collective-permute-start | bytes 589832 | tf_op jit(solution)/shard_map/ppermute | solution.py:164
  191.6 10.0 %collective-permute-start.32 = (f32[192,256]{1,0:T(8,128)S(1)}, f32[192,256]{1,0:T(8,128)S(1)}, u32[]{:S(2)}, u32[]{:S(2)}) collective-permute-start(f32[192,256]{1,0:T(8,128)S(1)} %get-tuple-element.177), channel_id=1, source_target_pairs={{0,4},{1,5},{2,6},{3,7},{4,0},{5,1},{6,2},{7,3},{8,12},{9,13},{10,... | collective-permute-start | bytes 589832 | tf_op jit(solution)/shard_map/ppermute | solution.py:164
  192.3 9.9 %collective-permute-start.33 = (f32[192,256]{1,0:T(8,128)S(1)}, f32[192,256]{1,0:T(8,128)S(1)}, u32[]{:S(2)}, u32[]{:S(2)}) collective-permute-start(f32[192,256]{1,0:T(8,128)S(1)} %get-tuple-element.176), channel_id=1, source_target_pairs={{0,12},{1,13},{2,14},{3,15},{4,8},{5,9},{6,10},{7,11},{8,4},{9,5},... | collective-permute-start | bytes 589832 | tf_op jit(solution)/shard_map/ppermute | solution.py:164
  193.0 9.3 %collective-permute-start.30 = (f32[768,128]{1,0:T(8,128)S(1)}, f32[768,128]{1,0:T(8,128)S(1)}, u32[]{:S(2)}, u32[]{:S(2)}) collective-permute-start(f32[768,128]{1,0:T(8,128)S(1)} %slice.143), channel_id=1, source_target_pairs={{0,1},{1,0},{2,3},{3,2},{4,5},{5,4},{6,7},{7,6},{8,9},{9,8},{10,11... | collective-permute-start | bytes 1179656 | tf_op jit(solution)/shard_map/ppermute | solution.py:164
  202.4 8.6 %collective-permute-start.37 = (f32[96,640]{1,0:T(8,128)S(1)}, f32[96,640]{1,0:T(8,128)S(1)}, u32[]{:S(2)}, u32[]{:S(2)}) collective-permute-start(f32[96,640]{1,0:T(8,128)S(1)} %slice.167), channel_id=1, source_target_pairs={{0,2},{1,3},{2,0},{3,1},{4,6},{5,7},{6,4},{7,5},{8,10},{9,11},{10,... | collective-permute-start | bytes 737288 | tf_op jit(solution)/shard_map/ppermute | solution.py:164
  204.9 9.4 %collective-permute-start.34 = (f32[192,384]{1,0:T(8,128)S(1)}, f32[192,384]{1,0:T(8,128)S(1)}, u32[]{:S(2)}, u32[]{:S(2)}) collective-permute-start(f32[192,384]{1,0:T(8,128)S(1)} %pad_maximum_fusion.4), channel_id=1, source_target_pairs={{0,8},{1,9},{2,10},{3,11},{4,12},{5,13},{6,14},{7,15},{8,0},{9,1},... | collective-permute-start | bytes 884744 | tf_op jit(solution)/shard_map/ppermute | solution.py:164
  207.0 9.2 %collective-permute-start.35 = (f32[192,128]{1,0:T(8,128)S(1)}, f32[192,128]{1,0:T(8,128)S(1)}, u32[]{:S(2)}, u32[]{:S(2)}) collective-permute-start(f32[192,128]{1,0:T(8,128)S(1)} %get-tuple-element.180), channel_id=1, source_target_pairs={{0,4},{1,5},{2,6},{3,7},{4,0},{5,1},{6,2},{7,3},{8,12},{9,13},{10,... | collective-permute-start | bytes 294920 | tf_op jit(solution)/shard_map/ppermute | solution.py:164
  207.7 9.8 %collective-permute-start.36 = (f32[192,128]{1,0:T(8,128)S(1)}, f32[192,128]{1,0:T(8,128)S(1)}, u32[]{:S(2)}, u32[]{:S(2)}) collective-permute-start(f32[192,128]{1,0:T(8,128)S(1)} %get-tuple-element.179), channel_id=1, source_target_pairs={{0,12},{1,13},{2,14},{3,15},{4,8},{5,9},{6,10},{7,11},{8,4},{9,5},... | collective-permute-start | bytes 294920 | tf_op jit(solution)/shard_map/ppermute | solution.py:164
  211.1 7.5 %copy-start.5 = (s32[8]{0:T(128)S(1)}, s32[8]{0:T(128)}, u32[]{:S(2)}) copy-start(s32[8]{0:T(128)} %constant.122.clone) | copy-start | bytes 100
  211.1 13.2 %copy-start.8 = (f32[512]{0:T(512)S(1)}, f32[512]{0:T(512)}, u32[]{:S(2)}) copy-start(f32[512]{0:T(512)} %param.10) | copy-start | bytes 6148
  217.6 6.8 %collective-permute-start.38 = (f32[96,384]{1,0:T(8,128)S(1)}, f32[96,384]{1,0:T(8,128)S(1)}, u32[]{:S(2)}, u32[]{:S(2)}) collective-permute-start(f32[96,384]{1,0:T(8,128)S(1)} %slice.169), channel_id=1, source_target_pairs={{0,2},{1,3},{2,0},{3,1},{4,6},{5,7},{6,4},{7,5},{8,10},{9,11},{10,... | collective-permute-start | bytes 442376 | tf_op jit(solution)/shard_map/ppermute | solution.py:164
  224.5 0.7 copy-start.7
